TPU v7x, 256 devices: a whole 4x4x8 slice. The times are simulated.
256 devices in a mesh: pair: 16 (over z, x_hi), ctx: 16 (over x_lo, y, core).
Axes of the slice: x: 4 (x_hi: 2, x_lo: 2; x = x_hi * 2 + x_lo), y: 4, z: 8, core: 2. Of those that a mesh axis runs over, the one named last changes fastest.
Arguments:
- queries: bfloat16 [16, 8192, 1024], P('pair', 'ctx'), may hold values from -6 to 6
- keys_values: bfloat16 [16, 8192, 256], P('pair', 'ctx'), may hold values from -6 to 6
- grad_out: bfloat16 [16, 8192, 1024], P('pair', 'ctx'), may hold values from -6 to 6
- log_norms: float32 [16, 8, 8192], P('pair', None, 'ctx'), may hold values from 3 to 8
- out_dots: float32 [16, 8, 8192], P('pair', None, 'ctx'), may hold values from -6 to 6
- doc_ids: int32 [16, 8192], P('pair'), may hold values from 0 to 8191, as said below
Outputs:
- grad_queries: bfloat16 [16, 8192, 1024], P('pair', 'ctx')
- grad_keys_values: bfloat16 [16, 8192, 256], P('pair', 'ctx')
Inputs may be any that keep to these rules, and one draw needn't show every extreme that they name: `doc_ids`: in each pack a token's document number is the position of the first token of its document, so numbers never fall along the sequence and each document is a contiguous run; every pack has one of exactly 2048; the last token of every pack is a document of its own; a pack and the pack 16/2 away were matched so that documents of one of them are far longer on average than those of the other.
All inputs are finite; a program needn't handle non-finite values.
Results may differ from a plain program's by a relative error of at most 0.0049.
Values may be sent and summed in bfloat16 or wider, within the bound.
No kernel may reach another device: no remote copies, remote signals or barrier semaphores. Data moves between devices by JAX's collectives and lax.ppermute only.
A program may use at most 128 MiB of HBM per device.

v0:
```python
import math

import jax
import jax.numpy as jnp
from jax import lax
from jax.sharding import PartitionSpec as P


def tile_grads(rows, kv_block, key_docs, key_pos):
    q_rows, cot_rows, lse_rows, dot_rows, query_docs, query_pos = rows
    q_count = q_rows.shape[0]
    k_count = kv_block.shape[0]
    head_dim = kv_block.shape[1] // 2
    head_count = q_rows.shape[1] // head_dim
    score_scale = head_dim ** (-0.5)
    allowed = (query_docs[:, None] == key_docs[None, :]) & (key_pos[None, :] <= query_pos[:, None])

    def live(unused):
        query_heads = q_rows.reshape(q_count, head_count, head_dim)
        cot_heads = cot_rows.reshape(q_count, head_count, head_dim)
        key_part = kv_block[:, :head_dim]
        value_part = kv_block[:, head_dim:]
        scores = (
            jnp.einsum("qhd,kd->hqk", query_heads, key_part, preferred_element_type=jnp.float32)
            * score_scale
        )
        probs = jnp.where(allowed[None], jnp.exp(scores - lse_rows[:, :, None]), jnp.float32(0.0))
        prob_grad = jnp.einsum(
            "qhd,kd->hqk", cot_heads, value_part, preferred_element_type=jnp.float32
        )
        score_grad = probs * (prob_grad - dot_rows[:, :, None])
        probs_low = probs.astype(jnp.bfloat16)
        score_low = score_grad.astype(jnp.bfloat16)
        query_grad = (
            jnp.einsum("hqk,kd->qhd", score_low, key_part, preferred_element_type=jnp.float32)
            * score_scale
        )
        key_grad = (
            jnp.einsum("hqk,qhd->kd", score_low, query_heads, preferred_element_type=jnp.float32)
            * score_scale
        )
        value_grad = jnp.einsum(
            "hqk,qhd->kd", probs_low, cot_heads, preferred_element_type=jnp.float32
        )
        return (
            query_grad.reshape(q_count, head_count * head_dim),
            jnp.concatenate([key_grad, value_grad], axis=1),
        )

    def dead(unused):
        return (
            jnp.zeros((q_count, q_rows.shape[1]), jnp.float32),
            jnp.zeros((k_count, 2 * head_dim), jnp.float32),
        )

    return lax.cond(jnp.any(allowed), live, dead, 0)


def sweep_keys(rows, kv_rows, key_docs_all, query_grad, kv_grad):
    k_total = kv_rows.shape[0]
    block_width = math.gcd(k_total, 512)
    block_count = k_total // block_width

    def advance(index_block, running):
        query_acc, kv_acc = running
        offset = index_block * block_width
        kv_block = lax.dynamic_slice_in_dim(kv_rows, offset, block_width, 0)
        key_docs = lax.dynamic_slice_in_dim(key_docs_all, offset, block_width, 0)
        key_pos = offset + jnp.arange(block_width, dtype=jnp.int32)
        query_part, kv_part = tile_grads(rows, kv_block, key_docs, key_pos)
        current = lax.dynamic_slice_in_dim(kv_acc, offset, block_width, 0)
        kv_acc = lax.dynamic_update_slice_in_dim(kv_acc, current + kv_part, offset, 0)
        return (query_acc + query_part, kv_acc)

    return lax.fori_loop(0, block_count, advance, (query_grad, kv_grad))


def per_device(queries, keys_values, grad_out, log_norms, out_dots, doc_ids):
    tok_rows = queries.shape[1]
    q_width = queries.shape[2]
    kv_width = keys_values.shape[2]
    doc_row = doc_ids[0]
    seq_len = doc_row.shape[0]
    q_first = lax.axis_index("ctx") * tok_rows
    local_pos = jnp.arange(tok_rows, dtype=jnp.int32)
    query_docs = lax.dynamic_slice_in_dim(doc_row, q_first, tok_rows, 0)
    empty_kv = jnp.zeros((seq_len, kv_width), jnp.float32)
    all_rows = (
        queries[0, 0:tok_rows],
        grad_out[0, 0:tok_rows],
        log_norms[0],
        out_dots[0],
        query_docs,
        q_first + local_pos,
    )
    empty_q = jnp.zeros((tok_rows, q_width), jnp.float32)
    kv_block = lax.all_gather(keys_values, "ctx", axis=1, tiled=True)[0]
    query_grad, kv_grad = sweep_keys(all_rows, kv_block, doc_row, empty_q, empty_kv)
    kv_share = lax.psum_scatter(kv_grad[None], "ctx", scatter_dimension=1, tiled=True)
    return (query_grad.astype(jnp.bfloat16)[None], kv_share.astype(jnp.bfloat16))


def solution(mesh):
    in_specs = (
        P("pair", "ctx", None),
        P("pair", "ctx", None),
        P("pair", "ctx", None),
        P("pair", None, "ctx"),
        P("pair", None, "ctx"),
        P("pair", None),
    )
    out_specs = (P("pair", "ctx", None), P("pair", "ctx", None))
    return jax.shard_map(
        per_device, mesh=mesh, in_specs=in_specs, out_specs=out_specs, check_vma=False
    )
```

profile of v0, /device:TPU:32, one launch (start us, length us, event | category | flops | bytes accessed | tf_op | source)
XLA Modules:
  0.0 592.2 jit_solution(4762517791406387597)
XLA Ops:
  9.5 2.3 copy.15
  12.4 40.0 %all-gather.2.cloned.1.call-done = bf16[1,8192,256]{2,1,0:T(8,128)(2,1)} async-done(((bf16[1,512,256]{2,1,0:T(8,128)(2,1)}), bf16[1,8192,256]{2,1,0:T(8,128)(2,1)}) %all-gather.2.cloned.1.call-update) | async-done | bytes 4194320 | tf_op jit(solution)/shard_map/all_gather | solution.py:97
  52.4 3.8 broadcast_in_dim.36.clone
  56.2 286.4 %while.16 = (s32[]{:T(128)}, f32[512,1024]{0,1:T(8,128)}, f32[8192,256]{1,0:T(8,128)}, s32[512]{0:T(512)S(1)}, s32[8192]{0:T(1024)}, /*index=5*/bf16[8192,256]{1...) while((s32[]{:T(128)}, f32[512,1024]{0,1:T(8,128)}, ...), condition=%wide.region_4.5_spmd.clone, body=%wide.region_0.4_spmd.clone.sunk | while | flops 2708276224 | bytes 96668016 | solution.py:75
  58.6 16.5 %conditional.3 = (f32[512,1024]{0,1:T(8,128)S(1)}, f32[512,256]{0,1:T(8,128)}) conditional(s32[]{:T(128)} %convert_element_type.31, () %tuple.57, (pred[512,512]{0,1:T(8,128)(4,1)S(1)}, bf16[8192,256]{1,0:T(8,128)(2,1)}, s32[]{:T(128)}, bf16[1,512,1024]{1,2,0:T(8,128)(2,1)S(1)}, f32[1,8,512]{2,1,0:T(8,128)S(1)}, ...), branch_computations={%region_2.0_spmd, %region_3.3_spmd} | conditional | flops 2706046976 | bytes 84330072 | solution.py:56
  58.6 5.5 fusion.14
  64.1 5.0 fusion.3
  77.0 2.1 copy.30
  79.1 2.1 add.101
  92.4 2.1 copy.30
  94.5 2.1 add.101
  100.6 3.4 select_add_fusion.2
  109.5 2.1 copy.30
  111.6 2.1 add.101
  117.7 3.4 select_add_fusion.2
  126.5 2.1 copy.30
  128.6 2.1 add.101
  134.7 3.4 select_add_fusion.2
  143.6 2.1 copy.30
  145.7 2.1 add.101
  151.7 3.4 select_add_fusion.2
  160.6 2.1 copy.30
  162.7 2.1 add.101
  168.8 3.4 select_add_fusion.2
  177.6 2.1 copy.30
  179.7 2.1 add.101
  185.8 3.4 select_add_fusion.2
  194.7 2.1 copy.30
  196.8 2.1 add.101
  202.8 3.4 select_add_fusion.2
  213.8 2.1 add.101
  219.9 3.4 select_add_fusion.2
  228.7 2.1 copy.30
  230.8 2.1 add.101
  236.9 3.4 select_add_fusion.2
  247.8 2.1 add.101
  254.0 3.4 select_add_fusion.2
  264.9 2.1 add.101
  271.0 3.4 select_add_fusion.2
  281.9 2.1 add.101
  288.0 3.4 select_add_fusion.2
  299.0 2.1 add.101
  305.1 3.4 select_add_fusion.2
  316.0 2.1 add.101
  322.1 3.4 select_add_fusion.2
  333.1 2.1 add.101
  339.2 3.4 select_add_fusion.2
  345.6 238.0 %reduce-scatter.2.cloned.1.call-done = f32[1,512,256]{2,1,0:T(8,128)} async-done(((f32[1,8192,256]{2,1,0:T(8,128)}), f32[1,512,256]{2,1,0:T(8,128)}) %reduce-scatter.2.cloned.1.call-update) | async-done | bytes 524304 | tf_op jit(solution)/shard_map/reduce_scatter | solution.py:99
  (172 shorter events, 186.2 us)
Async XLA Ops:
  7.2 45.2 %all-gather.2.cloned.1.call-start = ((), (), s32[]{:S(2)}) async-start(), calls=%async_computation.1 | async-start | bytes 4456448 | tf_op jit(solution)/shard_map/all_gather | solution.py:97
  7.9 575.7 %reduce-scatter.2.cloned.1.call-start = ((), (), s32[]{:S(2)}) async-start(), calls=%async_computation.2 | async-start | bytes 8912896 | tf_op jit(solution)/shard_map/reduce_scatter | solution.py:99
  52.4 3.8 copy-start.3
  52.4 3.8 copy-start.4
  58.6 5.5 copy-start.2
  64.1 6.5 %copy-start = (f32[512,512,8]{1,0,2:T(8,128)S(1)}, f32[512,512,8]{1,0,2:T(8,128)}, u32[]{:S(2)}) copy-start(f32[512,512,8]{1,0,2:T(8,128)} %fusion.14) | copy-start | bytes 25165828 | tf_op jit(solution)/shard_map/while/body/eval_jaxpr/cond
  342.6 1.6 copy-start.1
Sparse Core Ops, SparseCore 0:
  9.8 42.5 all-gather.1
  342.8 240.8 reduce-scatter.1
where the time goes:
time: 597 us; the launch traced here: 592 us
  waiting for transfers between devices  279 us (47%)
  local copies, waits for them, and re-layouts  168 us (28%)
  other arithmetic  106 us (18%)
  matrix products  15.6 us (3%)
  between operations  14.1 us (2%)
  loops' own time  10.5 us (2%)
    reduce_scatter x1, waiting for transfers between devices, per_device(): lax.psum_scatter(kv_grad[None], 'ctx', scatter_dimension=1, tiled=True)  238 us
    dynamic_slice x32, local copies, waits for them, and re-layouts, advance(): current = lax.dynamic_slice_in_dim(kv_acc, offset, block_width, 0)  64.1 us
    dynamic_update_slice x32, local copies, waits for them, and re-layouts, advance(): lax.dynamic_update_slice_in_dim(kv_acc, current + kv_part, offset, 0)  63.4 us
    add x16, other arithmetic, advance(): return (query_acc + query_part, kv_acc)  53 us
    all_gather x1, waiting for transfers between devices, per_device(): kv_block = lax.all_gather(keys_values, 'ctx', axis=1, tiled=True)[0]  40 us
    add x16, other arithmetic, advance(): current + kv_part  34 us
    another operation x30, local copies, waits for them, and re-layouts  16.8 us
    reduce_or x16, other arithmetic, tile_grads(): return lax.cond(jnp.any(allowed), live, dead, 0)  15.9 us
  transfers between devices with their start and end apart: 2, of which 2 were waited for; matrix products, arithmetic and copies ran while one was open for 1% of the time, Pallas kernels for 0%

commit v1 on v0

v1 whole, which is shorter than its diff:
```python
import functools
import math

import jax
import jax.numpy as jnp
from jax import lax
from jax.experimental import pallas as pl
from jax.experimental.pallas import tpu as pltpu
from jax.sharding import PartitionSpec as P

F32 = jnp.float32
BF16 = jnp.bfloat16
LOG2E = math.log2(math.e)
ROWS = 256
MIB = 1 << 20


def dot(a, b, dim_a, dim_b):
    return lax.dot_general(a, b, (((dim_a,), (dim_b,)), ((), ())), preferred_element_type=F32)


def attend(q, cot, lse, dots, lo, kpos, qpos, kv_ref, kt_ref, acc_ref, dkv_ref, first):
    head_dim = kt_ref.shape[0]
    heads = q.shape[1] // head_dim
    scale = head_dim**-0.5
    keys = kv_ref.shape[0]
    rows = q.shape[0]
    key = kpos + lax.broadcasted_iota(jnp.int32, (keys, rows), 0)
    query = qpos + lax.broadcasted_iota(jnp.int32, (1, rows), 1)
    allowed = (key >= lo) & (key <= query)
    lse2 = lse * LOG2E
    k = kv_ref[:, :head_dim]
    v = kv_ref[:, head_dim:]
    dk = jnp.zeros((keys, head_dim), F32)
    dv = jnp.zeros((keys, head_dim), F32)
    for h in range(heads):
        cols = slice(h * head_dim, (h + 1) * head_dim)
        qh = q[:, cols]
        oh = cot[:, cols]
        scores = dot(k, qh, 1, 1)
        prob_grad = dot(v, oh, 1, 1)
        probs = jnp.where(allowed, jnp.exp2(scores * (scale * LOG2E) - lse2[h : h + 1]), 0.0)
        score_low = (probs * (prob_grad - dots[h : h + 1])).astype(BF16)
        probs_low = probs.astype(BF16)
        dv += dot(probs_low, oh, 1, 0)
        dk += dot(score_low, qh, 1, 0)
        part = dot(kt_ref[...], score_low, 1, 0)
        acc_ref[h] = part if first else acc_ref[h] + part
    dkv_ref[:, :head_dim] += dk * scale
    dkv_ref[:, head_dim:] += dv


def near_kernel(other, place_ref, docs_ref, lo_ref, lse_ref, dots_ref, q_ref, cot_ref, kv_ref, *rest):
    if other:
        dkv_in, _, acc_ref, dkv_ref, kt, acc, sems = rest
    else:
        acc_ref, dkv_ref, kt, acc, sems = rest
    keys = kv_ref.shape[0]
    core = place_ref[1]
    chip_pos = place_ref[0] * (2 * keys)
    kpos = chip_pos + core * keys
    block = 1 - core if other else core
    dkv_ref[...] = dkv_in[...] if other else jnp.zeros_like(dkv_ref)
    kt[...] = kv_ref[:, : kt.shape[0]].T
    per = keys // ROWS
    for g in range(per):
        at = block * per + g
        qpos = pl.multiple_of(chip_pos + at * ROWS, ROWS)
        live = (docs_ref[0, qpos] < kpos + keys) & (qpos + ROWS > kpos)
        rows = slice(g * ROWS, (g + 1) * ROWS)

        @pl.when(live)
        def _():
            attend(q_ref[rows], cot_ref[rows], lse_ref[:, rows], dots_ref[:, rows],
                   lo_ref[0:1, pl.ds(qpos, ROWS)], kpos, qpos, kv_ref, kt, acc.at[g], dkv_ref, True)

        @pl.when(jnp.logical_not(live))
        def _():
            acc[g] = jnp.zeros_like(acc[g])

        pltpu.make_async_copy(acc.at[g], acc_ref.at[at], sems.at[g]).start()
    for g in range(per):
        pltpu.make_async_copy(acc.at[g], acc_ref.at[block * per + g], sems.at[g]).wait()


def far_kernel(chips, place_ref, docs_ref, lo_ref, lse_ref, dots_ref, stat_ref, q_ref, cot_ref,
               q2_ref, cot2_ref, kv_hbm, _, acc_ref, dkv_ref, kv, kt, q, cot, acc, dkv,
               kv_sem, q_sem, cot_sem, in_sem, out_sem):
    keys = kv.shape[0]
    core = place_ref[1]
    chip_pos = place_ref[0] * (2 * keys)
    kpos = (place_ref[0] - chips) * (2 * keys) + core * keys
    per = keys // ROWS
    total = 2 * per
    count = 0
    for g in range(total):
        live = (docs_ref[0, chip_pos + g * ROWS] < kpos + keys) & (kpos >= 0)
        count = count + live.astype(jnp.int32)
    dkv[...] = jnp.zeros_like(dkv)

    def begin(g, unused):
        own = (g // per) == core
        rows = pl.ds(pl.multiple_of((g % per) * ROWS, ROWS), ROWS)

        @pl.when(own)
        def _():
            pltpu.make_async_copy(q_ref.at[rows], q.at[g], q_sem.at[g]).start()
            pltpu.make_async_copy(cot_ref.at[rows], cot.at[g], cot_sem.at[g]).start()

        @pl.when(jnp.logical_not(own))
        def _():
            pltpu.make_async_copy(q2_ref.at[rows], q.at[g], q_sem.at[g]).start()
            pltpu.make_async_copy(cot2_ref.at[rows], cot.at[g], cot_sem.at[g]).start()

        pltpu.make_async_copy(acc_ref.at[g], acc.at[g], in_sem.at[g]).start()
        return unused

    @pl.when(count > 0)
    def _():
        pltpu.make_async_copy(kv_hbm, kv, kv_sem).start()
        lax.fori_loop(0, count, begin, 0)
        pltpu.make_async_copy(kv_hbm, kv, kv_sem).wait()
        kt[...] = kv[:, : kt.shape[0]].T

    def step(g, unused):
        own = (g // per) == core
        cols = pl.ds(pl.multiple_of((g % per) * ROWS, ROWS), ROWS)
        some = pl.ds(0, ROWS)
        pltpu.make_async_copy(q_ref.at[some], q.at[g], q_sem.at[g]).wait()
        pltpu.make_async_copy(cot_ref.at[some], cot.at[g], cot_sem.at[g]).wait()
        pltpu.make_async_copy(acc_ref.at[g], acc.at[g], in_sem.at[g]).wait()
        qpos = pl.multiple_of(chip_pos + g * ROWS, ROWS)
        lse = jnp.where(own, lse_ref[:, cols], stat_ref[0, :, cols])
        dots = jnp.where(own, dots_ref[:, cols], stat_ref[1, :, cols])
        attend(q.at[g], cot.at[g], lse, dots, lo_ref[0:1, pl.ds(qpos, ROWS)], kpos, qpos,
               kv, kt, acc.at[g], dkv, False)
        pltpu.make_async_copy(acc.at[g], acc_ref.at[g], out_sem.at[g]).start()
        return unused

    def end(g, unused):
        pltpu.make_async_copy(acc.at[g], acc_ref.at[g], out_sem.at[g]).wait()
        return unused

    lax.fori_loop(0, count, step, 0)
    dkv_ref[...] = dkv[...].astype(dkv_ref.dtype)
    lax.fori_loop(0, count, end, 0)


def finish_kernel(place_ref, acc_hbm, got_ref, out_ref, acc, sems):
    per, heads, head_dim = got_ref.shape[:3]
    core = place_ref[1]
    scale = head_dim**-0.5
    copies = [
        pltpu.make_async_copy(acc_hbm.at[core * per + g], acc.at[g], sems.at[g]) for g in range(per)
    ]
    for copy in copies:
        copy.start()
    for g in range(per):
        copies[g].wait()
        for h in range(heads):
            part = (acc[g, h] + got_ref[g, h].astype(F32)) * scale
            out_ref[g * ROWS : (g + 1) * ROWS, h * head_dim : (h + 1) * head_dim] = part.T.astype(BF16)


def per_device(chips_ctx, queries, keys_values, grad_out, log_norms, out_dots, doc_ids):
    tok, width = queries.shape[1:]
    head_dim = keys_values.shape[2] // 2
    heads = width // head_dim
    seq = doc_ids.shape[1]
    per = tok // ROWS
    q, kv, cot, lse, dots = queries[0], keys_values[0], grad_out[0], log_norms[0], out_dots[0]
    me = lax.axis_index("ctx")
    place = jnp.stack([me // 2, me % 2]).astype(jnp.int32)
    n_dev = 2 * chips_ctx
    cores = [(i, i ^ 1) for i in range(n_dev)]
    reach = min(chips_ctx - 1, -(-(seq - 2048 - 2) // (2 * tok)))

    q2 = lax.ppermute(q, "ctx", cores)
    cot2 = lax.ppermute(cot, "ctx", cores)
    stat2 = lax.ppermute(jnp.stack([lse, dots]), "ctx", cores)
    far_kv = [
        lax.ppermute(kv, "ctx", [(i, i + 2 * d) for i in range(n_dev - 2 * d)])
        for d in range(1, reach + 1)
    ]

    smem = pl.BlockSpec(memory_space=pltpu.SMEM)
    vmem = pl.BlockSpec(memory_space=pltpu.VMEM)
    hbm = pl.BlockSpec(memory_space=pl.ANY)
    acc_shape = jax.ShapeDtypeStruct((2 * per, heads, head_dim, ROWS), F32)
    tile_flops = 5 * 2 * tok * tok * width
    params = pltpu.CompilerParams(vmem_limit_bytes=40 * MIB)

    def cost(tiles):
        return pl.CostEstimate(flops=int(2 * tiles * tile_flops), bytes_accessed=4 * MIB, transcendentals=0)

    near_scratch = [
        pltpu.VMEM((head_dim, tok), BF16),
        pltpu.VMEM((per, heads, head_dim, ROWS), F32),
        pltpu.SemaphoreType.DMA((per,)),
    ]
    acc, dkv0 = pl.pallas_call(
        functools.partial(near_kernel, False),
        out_shape=(acc_shape, jax.ShapeDtypeStruct((tok, 2 * head_dim), F32)),
        in_specs=[smem, smem] + [vmem] * 6,
        out_specs=(hbm, vmem),
        scratch_shapes=near_scratch,
        compiler_params=params,
        cost_estimate=cost(1),
        name="own_queries",
    )(place, doc_ids, doc_ids, lse, dots, q, cot, kv)
    acc, dkv0 = pl.pallas_call(
        functools.partial(near_kernel, True),
        out_shape=(acc_shape, jax.ShapeDtypeStruct((tok, 2 * head_dim), F32)),
        in_specs=[smem, smem] + [vmem] * 7 + [hbm],
        out_specs=(hbm, vmem),
        scratch_shapes=near_scratch,
        input_output_aliases={9: 0},
        compiler_params=params,
        cost_estimate=cost(1),
        name="other_core",
    )(place, doc_ids, doc_ids, stat2[0], stat2[1], q2, cot2, kv, dkv0, acc)

    sent = []
    for d in range(1, reach + 1):
        acc, part = pl.pallas_call(
            functools.partial(far_kernel, d),
            out_shape=(acc_shape, jax.ShapeDtypeStruct((tok, 2 * head_dim), BF16)),
            in_specs=[smem, smem] + [vmem] * 4 + [hbm] * 6,
            out_specs=(hbm, vmem),
            scratch_shapes=[
                pltpu.VMEM((tok, 2 * head_dim), BF16),
                pltpu.VMEM((head_dim, tok), BF16),
                pltpu.VMEM((2 * per, ROWS, width), BF16),
                pltpu.VMEM((2 * per, ROWS, width), BF16),
                pltpu.VMEM((2 * per, heads, head_dim, ROWS), F32),
                pltpu.VMEM((tok, 2 * head_dim), F32),
                pltpu.SemaphoreType.DMA,
                pltpu.SemaphoreType.DMA((2 * per,)),
                pltpu.SemaphoreType.DMA((2 * per,)),
                pltpu.SemaphoreType.DMA((2 * per,)),
                pltpu.SemaphoreType.DMA((2 * per,)),
            ],
            input_output_aliases={11: 0},
            compiler_params=params,
            cost_estimate=cost(2),
            name=f"back_{d}",
        )(place, doc_ids, doc_ids, lse, dots, stat2, q, cot, q2, cot2, far_kv[d - 1], acc)
        sent.append(lax.ppermute(part, "ctx", [(i + 2 * d, i) for i in range(n_dev - 2 * d)]))

    core = me % 2
    give = lax.dynamic_slice_in_dim(acc, (1 - core) * per, per, 0).astype(BF16)
    got = lax.ppermute(give, "ctx", cores)
    grad_q = pl.pallas_call(
        finish_kernel,
        out_shape=jax.ShapeDtypeStruct((tok, width), BF16),
        in_specs=[smem, hbm, vmem],
        out_specs=vmem,
        scratch_shapes=[
            pltpu.VMEM((per, heads, head_dim, ROWS), F32),
            pltpu.SemaphoreType.DMA((per,)),
        ],
        compiler_params=params,
        name="finish",
    )(place, acc, got)
    grad_kv = dkv0
    for part in sent:
        grad_kv = grad_kv + part.astype(F32)
    return grad_q[None], grad_kv.astype(BF16)[None]


def solution(mesh):
    in_specs = (
        P("pair", "ctx", None),
        P("pair", "ctx", None),
        P("pair", "ctx", None),
        P("pair", None, "ctx"),
        P("pair", None, "ctx"),
        P("pair", None),
    )
    out_specs = (P("pair", "ctx", None), P("pair", "ctx", None))
    return jax.shard_map(
        functools.partial(per_device, mesh.shape["ctx"] // 2),
        mesh=mesh, in_specs=in_specs, out_specs=out_specs, check_vma=False,
    )
```

time: 597 us -> 112 us (0.19)
  waiting for transfers between devices: 279 us -> 38.3 us
  local copies, waits for them, and re-layouts: 168 us -> 18.2 us
  other arithmetic: 106 us -> 1.74 us
  Pallas kernels: 0 us -> 25.8 us
  starting transfers between devices: 0.08 us -> 24.7 us
  matrix products: 15.6 us -> 0 us
  between operations: 14.1 us -> 1.18 us
  loops' own time: 10.5 us -> 0 us
    reduce_scatter x1 -> x0, waiting for transfers between devices: 238 us -> none  [per_device(): lax.psum_scatter(kv_grad[None], 'ctx', scatter_dimension=1, tiled=True)]
    add x48 -> x0, other arithmetic: 87.1 us -> none  [the longest x16 53 us: advance(): return (query_acc + query_part, kv_acc)]
    dynamic_slice x49 -> x0, local copies, waits for them, and re-layouts: 77 us -> none  [the longest x32 64.1 us: advance(): current = lax.dynamic_slice_in_dim(kv_acc, offset, block_width, 0)]
    dynamic_update_slice x32 -> x0, local copies, waits for them, and re-layouts: 63.4 us -> none  [advance(): lax.dynamic_update_slice_in_dim(kv_acc, current + kv_part, offset, 0)]
    all_gather x1 -> x0, waiting for transfers between devices: 40 us -> none  [per_device(): kv_block = lax.all_gather(keys_values, 'ctx', axis=1, tiled=True)[0]]
    ppermute x0 -> x16, waiting for transfers between devices: none -> 38.3 us  [the longest x6 38.2 us: per_device(): lax.ppermute(part, 'ctx', [(i + 2 * d, i) for i in range(n_dev - 2 * d)])]
    pallas_call x0 -> x9, Pallas kernels: none -> 25.8 us  [the longest x6 8.25 us: per_device(): pl.pallas_call(functools.partial(far_kernel, d), out_shape=(acc_shape, ja...]
    ppermute x0 -> x16, starting transfers between devices: none -> 24.7 us  [the longest x6 16.4 us: per_device(): lax.ppermute(kv, 'ctx', [(i, i + 2 * d) for i in range(n_dev - 2 * d)])]
  transfers between devices with their start and end apart: 2 -> 16, of which waited for: 2 -> 4; matrix products, arithmetic and copies ran while one was open for 1% -> 2% of each run, Pallas kernels for 0% -> 20%
where the time goes in v1:
time: 112 us; the launch traced here: 110 us
  waiting for transfers between devices  38.3 us (34%)
  Pallas kernels  25.8 us (23%)
  starting transfers between devices  24.7 us (22%)
  local copies, waits for them, and re-layouts  18.2 us (16%)
  other arithmetic  1.74 us (2%)
  between operations  1.18 us (1%)
    ppermute x6, waiting for transfers between devices, per_device(): lax.ppermute(part, 'ctx', [(i + 2 * d, i) for i in range(n_dev - 2 * d)])  38.2 us
    unnamed x36, local copies, waits for them, and re-layouts  18.1 us
    ppermute x6, starting transfers between devices, per_device(): lax.ppermute(kv, 'ctx', [(i, i + 2 * d) for i in range(n_dev - 2 * d)])  16.4 us
    pallas_call x6, Pallas kernels, per_device(): pl.pallas_call(functools.partial(far_kernel, d), out_shape=(acc_shape, ja...  8.25 us
    pallas_call x1, Pallas kernels, per_device(): pl.pallas_call(functools.partial(near_kernel, True), out_shape=(acc_shape...  7.79 us
    ppermute x6, starting transfers between devices, per_device(): lax.ppermute(part, 'ctx', [(i + 2 * d, i) for i in range(n_dev - 2 * d)])  7.73 us
    pallas_call x1, Pallas kernels, per_device(): pl.pallas_call(functools.partial(near_kernel, False), out_shape=(acc_shap...  7.61 us
  transfers between devices with their start and end apart: 16, of which 4 were waited for; matrix products, arithmetic and copies ran while one was open for 2% of the time, Pallas kernels for 20%

profile of v1, /device:TPU:32, one launch (start us, length us, event | category | flops | bytes accessed | tf_op | source)
XLA Modules:
  0.0 109.9 jit_solution(5544945859549307971)
XLA Ops:
  0.6 0.1 collective-permute-start.1
  0.7 0.5 collective-permute-start.2
  1.2 3.5 %collective-permute-start.8 = (bf16[512,256]{1,0:T(8,128)(2,1)}, bf16[512,256]{1,0:T(8,128)(2,1)S(1)}, u32[]{:S(2)}, u32[]{:S(2)}) collective-permute-start(bf16[512,256]{1,0:T(8,128)(2,1)} %bitcast.44), channel_id=1, source_target_pairs={{0,2},{1,3},{2,4},{3,5},{4,6},{5,7},{6,8},{7,9},{8,10},{9,11},{10,... | collective-permute-start | bytes 786440 | tf_op jit(solution)/shard_map/ppermute | solution.py:182
  4.7 4.8 %collective-permute-start.7 = (bf16[512,256]{1,0:T(8,128)(2,1)}, bf16[512,256]{1,0:T(8,128)(2,1)S(1)}, u32[]{:S(2)}, u32[]{:S(2)}) collective-permute-start(bf16[512,256]{1,0:T(8,128)(2,1)} %bitcast.45), channel_id=1, source_target_pairs={{0,4},{1,5},{2,6},{3,7},{4,8},{5,9},{6,10},{7,11},{8,12},{9,13},{1... | collective-permute-start | bytes 786440 | tf_op jit(solution)/shard_map/ppermute | solution.py:182
  9.5 0.7 pad_maximum_fusion
  10.3 0.0 collective-permute-start
  10.3 0.1 pad_add_fusion.place_ref
  10.4 0.7 copy-done.6
  11.1 0.7 copy-done.8
  11.8 1.2 %copy-done.10 = bf16[1,512,1024]{2,1,0:T(8,128)(2,1)S(1)} copy-done((bf16[1,512,1024]{2,1,0:T(8,128)(2,1)S(1)}, bf16[1,512,1024]{2,1,0:T(8,128)(2,1)}, u32[]{:S(2)}) %copy-start.10) | copy-done | bytes 1048600
  13.0 1.2 %copy-done.12 = bf16[1,512,1024]{2,1,0:T(8,128)(2,1)S(1)} copy-done((bf16[1,512,1024]{2,1,0:T(8,128)(2,1)S(1)}, bf16[1,512,1024]{2,1,0:T(8,128)(2,1)}, u32[]{:S(2)}) %copy-start.12) | copy-done | bytes 1048600
  14.2 0.9 copy-done.14
  15.2 0.8 copy-done.16
  16.0 7.6 %own_queries.1 = (f32[4,8,128,256]{3,2,1,0:T(8,128)S(1)}, f32[512,256]{1,0:T(8,128)S(1)}) custom-call(s32[2]{0:T(128)S(1)} %pad_add_fusion.place_ref, s32[1,8192]{1,0:T(1,128)S(1)} %copy-done.16, s32[1,8192]{1,0:T(1,128)S(1)} %copy-done.16, f32[8,512]{1,0:T(8,128)S(1)} %bitcast.14, f32[8,512]{1,0:T(8,128)S(1)} %bitcast.21, bf16[512,1024]{1,0:T(8,128)(2,1)S(1)} %bitcast.29, ...), custom_call_target="tpu_custom_call" | custom-call | flops 5368709120 | bytes 4194304 | tf_op jit(solution)/shard_map/own_queries/pallas_call | solution.py:201
  23.6 2.0 %copy-done = f32[4,8,128,256]{3,2,1,0:T(8,128)} copy-done((f32[4,8,128,256]{3,2,1,0:T(8,128)}, f32[4,8,128,256]{3,2,1,0:T(8,128)S(1)}, u32[]{:S(2)}) %copy-start) | copy-done | bytes 4194328
  25.6 0.0 collective-permute-done.stat_ref
  25.6 4.2 %collective-permute-start.6 = (bf16[512,256]{1,0:T(8,128)(2,1)S(1)}, bf16[512,256]{1,0:T(8,128)(2,1)S(1)}, u32[]{:S(2)}, u32[]{:S(2)}) collective-permute-start(bf16[512,256]{1,0:T(8,128)(2,1)S(1)} %bitcast.47), channel_id=1, source_target_pairs={{0,6},{1,7},{2,8},{3,9},{4,10},{5,11},{6,12},{7,13},{8,14},{9,15},... | collective-permute-start | bytes 786440 | tf_op jit(solution)/shard_map/ppermute | solution.py:182
  29.8 1.3 %collective-permute-start.5 = (bf16[512,256]{1,0:T(8,128)(2,1)S(1)}, bf16[512,256]{1,0:T(8,128)(2,1)S(1)}, u32[]{:S(2)}, u32[]{:S(2)}) collective-permute-start(bf16[512,256]{1,0:T(8,128)(2,1)S(1)} %bitcast.48), channel_id=1, source_target_pairs={{0,8},{1,9},{2,10},{3,11},{4,12},{5,13},{6,14},{7,15},{16,24},{17,... | collective-permute-start | bytes 786440 | tf_op jit(solution)/shard_map/ppermute | solution.py:182
  31.1 0.0 collective-permute-done.2.cot_ref.cot2_ref
  31.1 1.3 %collective-permute-start.4 = (bf16[512,256]{1,0:T(8,128)(2,1)S(1)}, bf16[512,256]{1,0:T(8,128)(2,1)S(1)}, u32[]{:S(2)}, u32[]{:S(2)}) collective-permute-start(bf16[512,256]{1,0:T(8,128)(2,1)S(1)} %bitcast.49), channel_id=1, source_target_pairs={{0,10},{1,11},{2,12},{3,13},{4,14},{5,15},{16,26},{17,27},{18,28},... | collective-permute-start | bytes 786440 | tf_op jit(solution)/shard_map/ppermute | solution.py:182
  32.4 2.2 %copy-done.1 = f32[4,8,128,256]{3,2,1,0:T(8,128)S(1)} copy-done((f32[4,8,128,256]{3,2,1,0:T(8,128)S(1)}, f32[4,8,128,256]{3,2,1,0:T(8,128)}, u32[]{:S(2)}) %copy-start.1) | copy-done | bytes 4194328
  34.6 7.8 %other_core.1 = (f32[4,8,128,256]{3,2,1,0:T(8,128)S(1)}, f32[512,256]{1,0:T(8,128)S(1)}) custom-call(s32[2]{0:T(128)S(1)} %pad_add_fusion.place_ref, s32[1,8192]{1,0:T(1,128)S(1)} %copy-done.17, s32[1,8192]{1,0:T(1,128)S(1)} %copy-done.17, f32[8,512]{1,0:T(8,128)S(1)} %get-tuple-element.35.lse_ref, ...), custom_call_target="tpu_custom_call", output_to_operand_aliasing={{0}: (9, {})} | custom-call | flops 5368709120 | bytes 4194304 | tf_op jit(solution)/shard_map/other_core/pallas_call | solution.py:211
  42.4 2.0 %copy-done.2 = f32[4,8,128,256]{3,2,1,0:T(8,128)} copy-done((f32[4,8,128,256]{3,2,1,0:T(8,128)}, f32[4,8,128,256]{3,2,1,0:T(8,128)S(1)}, u32[]{:S(2)}) %copy-start.2) | copy-done | bytes 4194328
  44.4 1.3 %collective-permute-start.3 = (bf16[512,256]{1,0:T(8,128)(2,1)S(1)}, bf16[512,256]{1,0:T(8,128)(2,1)S(1)}, u32[]{:S(2)}, u32[]{:S(2)}) collective-permute-start(bf16[512,256]{1,0:T(8,128)(2,1)S(1)} %bitcast.51), channel_id=1, source_target_pairs={{0,12},{1,13},{2,14},{3,15},{16,28},{17,29},{18,30},{19,31},{32,44... | collective-permute-start | bytes 786440 | tf_op jit(solution)/shard_map/ppermute | solution.py:182
  45.8 2.2 %copy-done.3 = f32[4,8,128,256]{3,2,1,0:T(8,128)S(1)} copy-done((f32[4,8,128,256]{3,2,1,0:T(8,128)S(1)}, f32[4,8,128,256]{3,2,1,0:T(8,128)}, u32[]{:S(2)}) %copy-start.3) | copy-done | bytes 4194328
  47.9 1.3 %back_1.1 = (f32[4,8,128,256]{3,2,1,0:T(8,128)S(1)}, bf16[512,256]{1,0:T(8,128)(2,1)S(1)}) custom-call(s32[2]{0:T(128)S(1)} %pad_add_fusion.place_ref, s32[1,8192]{1,0:T(1,128)S(1)} %copy-done.17, s32[1,8192]{1,0:T(1,128)S(1)} %copy-done.17, f32[8,512]{1,0:T(8,128)S(1)} %bitcast.15, f32[8,512]{1,0:T(8,128)S(1)} %bitcast.22, ...), custom_call_target="tpu_custom_call", output_to_operand_aliasing={{0}: (11, {})} | custom-call | flops 10737418240 | bytes 4194304 | tf_op jit(solution)/shard_map/back_1/pallas_call | solution.py:225
  49.2 0.0 collective-permute-done.7.kv_hbm
  49.2 1.3 %back_2.1 = (f32[4,8,128,256]{3,2,1,0:T(8,128)S(1)}, bf16[512,256]{1,0:T(8,128)(2,1)S(1)}) custom-call(s32[2]{0:T(128)S(1)} %pad_add_fusion.place_ref, s32[1,8192]{1,0:T(1,128)S(1)} %copy-done.17, s32[1,8192]{1,0:T(1,128)S(1)} %copy-done.17, f32[8,512]{1,0:T(8,128)S(1)} %bitcast.16, f32[8,512]{1,0:T(8,128)S(1)} %bitcast.23, ...), custom_call_target="tpu_custom_call", output_to_operand_aliasing={{0}: (11, {})} | custom-call | flops 10737418240 | bytes 4194304 | tf_op jit(solution)/shard_map/back_2/pallas_call | solution.py:225
  50.5 0.0 collective-permute-done.6.kv_hbm
  50.6 1.5 %back_3.1 = (f32[4,8,128,256]{3,2,1,0:T(8,128)S(1)}, bf16[512,256]{1,0:T(8,128)(2,1)S(1)}) custom-call(s32[2]{0:T(128)S(1)} %pad_add_fusion.place_ref, s32[1,8192]{1,0:T(1,128)S(1)} %copy-done.17, s32[1,8192]{1,0:T(1,128)S(1)} %copy-done.17, f32[8,512]{1,0:T(8,128)S(1)} %bitcast.17, f32[8,512]{1,0:T(8,128)S(1)} %bitcast.24, ...), custom_call_target="tpu_custom_call", output_to_operand_aliasing={{0}: (11, {})} | custom-call | flops 10737418240 | bytes 4194304 | tf_op jit(solution)/shard_map/back_3/pallas_call | solution.py:225
  52.1 1.3 %back_4.1 = (f32[4,8,128,256]{3,2,1,0:T(8,128)S(1)}, bf16[512,256]{1,0:T(8,128)(2,1)S(1)}) custom-call(s32[2]{0:T(128)S(1)} %pad_add_fusion.place_ref, s32[1,8192]{1,0:T(1,128)S(1)} %copy-done.17, s32[1,8192]{1,0:T(1,128)S(1)} %copy-done.17, f32[8,512]{1,0:T(8,128)S(1)} %bitcast.18, f32[8,512]{1,0:T(8,128)S(1)} %bitcast.25, ...), custom_call_target="tpu_custom_call", output_to_operand_aliasing={{0}: (11, {})} | custom-call | flops 10737418240 | bytes 4194304 | tf_op jit(solution)/shard_map/back_4/pallas_call | solution.py:225
  53.4 1.3 %back_5.1 = (f32[4,8,128,256]{3,2,1,0:T(8,128)S(1)}, bf16[512,256]{1,0:T(8,128)(2,1)S(1)}) custom-call(s32[2]{0:T(128)S(1)} %pad_add_fusion.place_ref, s32[1,8192]{1,0:T(1,128)S(1)} %copy-done.17, s32[1,8192]{1,0:T(1,128)S(1)} %copy-done.17, f32[8,512]{1,0:T(8,128)S(1)} %bitcast.19, f32[8,512]{1,0:T(8,128)S(1)} %bitcast.26, ...), custom_call_target="tpu_custom_call", output_to_operand_aliasing={{0}: (11, {})} | custom-call | flops 10737418240 | bytes 4194304 | tf_op jit(solution)/shard_map/back_5/pallas_call | solution.py:225
  54.7 1.6 %back_6.1 = (f32[4,8,128,256]{3,2,1,0:T(8,128)S(1)}, bf16[512,256]{1,0:T(8,128)(2,1)S(1)}) custom-call(s32[2]{0:T(128)S(1)} %pad_add_fusion.place_ref, s32[1,8192]{1,0:T(1,128)S(1)} %copy-done.17, s32[1,8192]{1,0:T(1,128)S(1)} %copy-done.17, f32[8,512]{1,0:T(8,128)S(1)} %bitcast.20, f32[8,512]{1,0:T(8,128)S(1)} %bitcast.27, ...), custom_call_target="tpu_custom_call", output_to_operand_aliasing={{0}: (11, {})} | custom-call | flops 10737418240 | bytes 4194304 | tf_op jit(solution)/shard_map/back_6/pallas_call | solution.py:225
  56.3 0.1 dynamic-slice_convert_fusion
  56.4 2.0 %copy-done.4 = f32[4,8,128,256]{3,2,1,0:T(8,128)} copy-done((f32[4,8,128,256]{3,2,1,0:T(8,128)}, f32[4,8,128,256]{3,2,1,0:T(8,128)S(1)}, u32[]{:S(2)}) %copy-start.4) | copy-done | bytes 4194328
  58.4 1.3 %collective-permute-start.15 = (bf16[512,256]{1,0:T(8,128)(2,1)S(1)}, bf16[512,256]{1,0:T(8,128)(2,1)S(1)}, u32[]{:S(2)}, u32[]{:S(2)}) collective-permute-start(bf16[512,256]{1,0:T(8,128)(2,1)S(1)} %get-tuple-element.33), channel_id=1, source_target_pairs={{12,0},{13,1},{14,2},{15,3},{28,16},{29,17},{30,18},{31,19},{44,32... | collective-permute-start | bytes 786440 | tf_op jit(solution)/shard_map/ppermute | solution.py:248
  59.7 1.3 %collective-permute-start.14 = (bf16[512,256]{1,0:T(8,128)(2,1)S(1)}, bf16[512,256]{1,0:T(8,128)(2,1)S(1)}, u32[]{:S(2)}, u32[]{:S(2)}) collective-permute-start(bf16[512,256]{1,0:T(8,128)(2,1)S(1)} %get-tuple-element.32), channel_id=1, source_target_pairs={{10,0},{11,1},{12,2},{13,3},{14,4},{15,5},{26,16},{27,17},{28,18},... | collective-permute-start | bytes 786440 | tf_op jit(solution)/shard_map/ppermute | solution.py:248
  61.0 1.3 %collective-permute-start.13 = (bf16[512,256]{1,0:T(8,128)(2,1)S(1)}, bf16[512,256]{1,0:T(8,128)(2,1)S(1)}, u32[]{:S(2)}, u32[]{:S(2)}) collective-permute-start(bf16[512,256]{1,0:T(8,128)(2,1)S(1)} %get-tuple-element.31), channel_id=1, source_target_pairs={{8,0},{9,1},{10,2},{11,3},{12,4},{13,5},{14,6},{15,7},{24,16},{25,... | collective-permute-start | bytes 786440 | tf_op jit(solution)/shard_map/ppermute | solution.py:248
  62.3 1.3 %collective-permute-start.12 = (bf16[512,256]{1,0:T(8,128)(2,1)S(1)}, bf16[512,256]{1,0:T(8,128)(2,1)S(1)}, u32[]{:S(2)}, u32[]{:S(2)}) collective-permute-start(bf16[512,256]{1,0:T(8,128)(2,1)S(1)} %get-tuple-element.30), channel_id=1, source_target_pairs={{6,0},{7,1},{8,2},{9,3},{10,4},{11,5},{12,6},{13,7},{14,8},{15,9},... | collective-permute-start | bytes 786440 | tf_op jit(solution)/shard_map/ppermute | solution.py:248
  63.6 7.9 %collective-permute-done.15 = bf16[512,256]{1,0:T(8,128)(2,1)S(1)} collective-permute-done((bf16[512,256]{1,0:T(8,128)(2,1)S(1)}, bf16[512,256]{1,0:T(8,128)(2,1)S(1)}, u32[]{:S(2)}, u32[]{:S(2)}) %collective-permute-start.15) | collective-permute-done | bytes 262176 | tf_op jit(solution)/shard_map/ppermute | solution.py:248
  71.5 1.3 %collective-permute-start.11 = (bf16[512,256]{1,0:T(8,128)(2,1)S(1)}, bf16[512,256]{1,0:T(8,128)(2,1)S(1)}, u32[]{:S(2)}, u32[]{:S(2)}) collective-permute-start(bf16[512,256]{1,0:T(8,128)(2,1)S(1)} %get-tuple-element.29), channel_id=1, source_target_pairs={{4,0},{5,1},{6,2},{7,3},{8,4},{9,5},{10,6},{11,7},{12,8},{13,9},{1... | collective-permute-start | bytes 786440 | tf_op jit(solution)/shard_map/ppermute | solution.py:248
  72.8 1.3 %collective-permute-start.10 = (bf16[512,256]{1,0:T(8,128)(2,1)S(1)}, bf16[512,256]{1,0:T(8,128)(2,1)S(1)}, u32[]{:S(2)}, u32[]{:S(2)}) collective-permute-start(bf16[512,256]{1,0:T(8,128)(2,1)S(1)} %get-tuple-element.28), channel_id=1, source_target_pairs={{2,0},{3,1},{4,2},{5,3},{6,4},{7,5},{8,6},{9,7},{10,8},{11,9},{12,... | collective-permute-start | bytes 786440 | tf_op jit(solution)/shard_map/ppermute | solution.py:248
  74.1 2.9 %collective-permute-done.12 = bf16[512,256]{1,0:T(8,128)(2,1)S(1)} collective-permute-done((bf16[512,256]{1,0:T(8,128)(2,1)S(1)}, bf16[512,256]{1,0:T(8,128)(2,1)S(1)}, u32[]{:S(2)}, u32[]{:S(2)}) %collective-permute-start.12) | collective-permute-done | bytes 262176 | tf_op jit(solution)/shard_map/ppermute | solution.py:248
  77.0 5.7 %collective-permute-done.11 = bf16[512,256]{1,0:T(8,128)(2,1)S(1)} collective-permute-done((bf16[512,256]{1,0:T(8,128)(2,1)S(1)}, bf16[512,256]{1,0:T(8,128)(2,1)S(1)}, u32[]{:S(2)}, u32[]{:S(2)}) %collective-permute-start.11) | collective-permute-done | bytes 262176 | tf_op jit(solution)/shard_map/ppermute | solution.py:248
  82.8 21.7 %collective-permute-done.10 = bf16[512,256]{1,0:T(8,128)(2,1)S(1)} collective-permute-done((bf16[512,256]{1,0:T(8,128)(2,1)S(1)}, bf16[512,256]{1,0:T(8,128)(2,1)S(1)}, u32[]{:S(2)}, u32[]{:S(2)}) %collective-permute-start.10) | collective-permute-done | bytes 262176 | tf_op jit(solution)/shard_map/ppermute | solution.py:248
  104.5 0.9 fusion
  105.4 2.2 %copy-done.5 = f32[4,8,128,256]{3,2,1,0:T(8,128)S(1)} copy-done((f32[4,8,128,256]{3,2,1,0:T(8,128)S(1)}, f32[4,8,128,256]{3,2,1,0:T(8,128)}, u32[]{:S(2)}) %copy-start.5) | copy-done | bytes 4194328
  107.6 2.2 %finish.1 = bf16[512,1024]{1,0:T(8,128)(2,1)} custom-call(s32[2]{0:T(128)S(1)} %pad_add_fusion.place_ref, f32[4,8,128,256]{3,2,1,0:T(8,128)S(1)} %copy-done.5, bf16[2,8,128,256]{3,2,1,0:T(8,128)(2,1)S(1)} %collective-permute-done.9.got_ref), custom_call_target="tpu_custom_call" | custom-call | tf_op jit(solution)/shard_map/finish/pallas_call | solution.py:253
  (34 shorter events, 0.1 us)
Async XLA Ops:
  0.6 29.1 %collective-permute-start.1 = (bf16[512,1024]{1,0:T(8,128)(2,1)}, bf16[512,1024]{1,0:T(8,128)(2,1)S(1)}, u32[]{:S(2)}, u32[]{:S(2)}) collective-permute-start(bf16[512,1024]{1,0:T(8,128)(2,1)} %bitcast.28), channel_id=1, source_target_pairs={{0,1},{1,0},{2,3},{3,2},{4,5},{5,4},{6,7},{7,6},{8,9},{9,8},{10,11... | collective-permute-start | bytes 3145736 | tf_op jit(solution)/shard_map/ppermute | solution.py:178
  0.7 30.4 %collective-permute-start.2 = (bf16[512,1024]{1,0:T(8,128)(2,1)}, bf16[512,1024]{1,0:T(8,128)(2,1)S(1)}, u32[]{:S(2)}, u32[]{:S(2)}) collective-permute-start(bf16[512,1024]{1,0:T(8,128)(2,1)} %bitcast.36), channel_id=1, source_target_pairs={{0,1},{1,0},{2,3},{3,2},{4,5},{5,4},{6,7},{7,6},{8,9},{9,8},{10,11... | collective-permute-start | bytes 3145736 | tf_op jit(solution)/shard_map/ppermute | solution.py:179
  1.2 43.2 %collective-permute-start.8 = (bf16[512,256]{1,0:T(8,128)(2,1)}, bf16[512,256]{1,0:T(8,128)(2,1)S(1)}, u32[]{:S(2)}, u32[]{:S(2)}) collective-permute-start(bf16[512,256]{1,0:T(8,128)(2,1)} %bitcast.44), channel_id=1, source_target_pairs={{0,2},{1,3},{2,4},{3,5},{4,6},{5,7},{6,8},{7,9},{8,10},{9,11},{10,... | collective-permute-start | bytes 786440 | tf_op jit(solution)/shard_map/ppermute | solution.py:182
  4.7 44.5 %collective-permute-start.7 = (bf16[512,256]{1,0:T(8,128)(2,1)}, bf16[512,256]{1,0:T(8,128)(2,1)S(1)}, u32[]{:S(2)}, u32[]{:S(2)}) collective-permute-start(bf16[512,256]{1,0:T(8,128)(2,1)} %bitcast.45), channel_id=1, source_target_pairs={{0,4},{1,5},{2,6},{3,7},{4,8},{5,9},{6,10},{7,11},{8,12},{9,13},{1... | collective-permute-start | bytes 786440 | tf_op jit(solution)/shard_map/ppermute | solution.py:182
  10.3 15.3 %collective-permute-start = (f32[2,8,512]{2,1,0:T(8,128)S(1)}, f32[2,8,512]{2,1,0:T(8,128)S(1)}, u32[]{:S(2)}, u32[]{:S(2)}) collective-permute-start(f32[2,8,512]{2,1,0:T(8,128)S(1)} %pad_maximum_fusion), channel_id=1, source_target_pairs={{0,1},{1,0},{2,3},{3,2},{4,5},{5,4},{6,7},{7,6},{8,9},{9,8},{10,11... | collective-permute-start | bytes 98312 | tf_op jit(solution)/shard_map/ppermute | solution.py:180
  10.4 0.7 copy-start.6
  11.1 0.7 copy-start.8
  11.8 1.2 %copy-start.10 = (bf16[1,512,1024]{2,1,0:T(8,128)(2,1)S(1)}, bf16[1,512,1024]{2,1,0:T(8,128)(2,1)}, u32[]{:S(2)}) copy-start(bf16[1,512,1024]{2,1,0:T(8,128)(2,1)} %param.6) | copy-start | bytes 3145732
  13.0 1.2 %copy-start.12 = (bf16[1,512,1024]{2,1,0:T(8,128)(2,1)S(1)}, bf16[1,512,1024]{2,1,0:T(8,128)(2,1)}, u32[]{:S(2)}) copy-start(bf16[1,512,1024]{2,1,0:T(8,128)(2,1)} %param.8) | copy-start | bytes 3145732
  14.2 0.9 copy-start.14
  15.2 0.8 copy-start.16
  16.0 9.6 %copy-start.15 = (bf16[1,512,256]{2,1,0:T(8,128)(2,1)S(1)}, bf16[1,512,256]{2,1,0:T(8,128)(2,1)}, u32[]{:S(2)}) copy-start(bf16[1,512,256]{2,1,0:T(8,128)(2,1)} %param.7) | copy-start | bytes 786436
  16.0 16.5 %copy-start.17 = (s32[1,8192]{1,0:T(1,128)S(1)}, s32[1,8192]{1,0:T(1,128)}, u32[]{:S(2)}) copy-start(s32[1,8192]{1,0:T(1,128)} %lo_ref.15) | copy-start | bytes 98308
  23.6 2.0 %copy-start = (f32[4,8,128,256]{3,2,1,0:T(8,128)}, f32[4,8,128,256]{3,2,1,0:T(8,128)S(1)}, u32[]{:S(2)}) copy-start(f32[4,8,128,256]{3,2,1,0:T(8,128)S(1)} %get-tuple-element.19.rest_1_) | copy-start | bytes 12582916
  25.6 25.0 %collective-permute-start.6 = (bf16[512,256]{1,0:T(8,128)(2,1)S(1)}, bf16[512,256]{1,0:T(8,128)(2,1)S(1)}, u32[]{:S(2)}, u32[]{:S(2)}) collective-permute-start(bf16[512,256]{1,0:T(8,128)(2,1)S(1)} %bitcast.47), channel_id=1, source_target_pairs={{0,6},{1,7},{2,8},{3,9},{4,10},{5,11},{6,12},{7,13},{8,14},{9,15},... | collective-permute-start | bytes 786440 | tf_op jit(solution)/shard_map/ppermute | solution.py:182
  29.8 22.3 %collective-permute-start.5 = (bf16[512,256]{1,0:T(8,128)(2,1)S(1)}, bf16[512,256]{1,0:T(8,128)(2,1)S(1)}, u32[]{:S(2)}, u32[]{:S(2)}) collective-permute-start(bf16[512,256]{1,0:T(8,128)(2,1)S(1)} %bitcast.48), channel_id=1, source_target_pairs={{0,8},{1,9},{2,10},{3,11},{4,12},{5,13},{6,14},{7,15},{16,24},{17,... | collective-permute-start | bytes 786440 | tf_op jit(solution)/shard_map/ppermute | solution.py:182
  31.1 22.3 %collective-permute-start.4 = (bf16[512,256]{1,0:T(8,128)(2,1)S(1)}, bf16[512,256]{1,0:T(8,128)(2,1)S(1)}, u32[]{:S(2)}, u32[]{:S(2)}) collective-permute-start(bf16[512,256]{1,0:T(8,128)(2,1)S(1)} %bitcast.49), channel_id=1, source_target_pairs={{0,10},{1,11},{2,12},{3,13},{4,14},{5,15},{16,26},{17,27},{18,28},... | collective-permute-start | bytes 786440 | tf_op jit(solution)/shard_map/ppermute | solution.py:182
  32.4 2.2 %copy-start.1 = (f32[4,8,128,256]{3,2,1,0:T(8,128)S(1)}, f32[4,8,128,256]{3,2,1,0:T(8,128)}, u32[]{:S(2)}) copy-start(f32[4,8,128,256]{3,2,1,0:T(8,128)} %copy-done) | copy-start | bytes 12582916
  34.6 11.1 %copy-start.7 = (f32[1,8,512]{2,1,0:T(8,128)S(1)}, f32[1,8,512]{2,1,0:T(8,128)}, u32[]{:S(2)}) copy-start(f32[1,8,512]{2,1,0:T(8,128)} %param.9) | copy-start | bytes 49156
  34.6 11.1 %copy-start.9 = (f32[1,8,512]{2,1,0:T(8,128)S(1)}, f32[1,8,512]{2,1,0:T(8,128)}, u32[]{:S(2)}) copy-start(f32[1,8,512]{2,1,0:T(8,128)} %param.10) | copy-start | bytes 49156
  34.6 11.1 %copy-start.11 = (bf16[1,512,1024]{2,1,0:T(8,128)(2,1)S(1)}, bf16[1,512,1024]{2,1,0:T(8,128)(2,1)}, u32[]{:S(2)}) copy-start(bf16[1,512,1024]{2,1,0:T(8,128)(2,1)} %param.6) | copy-start | bytes 3145732
  34.6 11.1 %copy-start.13 = (bf16[1,512,1024]{2,1,0:T(8,128)(2,1)S(1)}, bf16[1,512,1024]{2,1,0:T(8,128)(2,1)}, u32[]{:S(2)}) copy-start(bf16[1,512,1024]{2,1,0:T(8,128)(2,1)} %param.8) | copy-start | bytes 3145732
  42.4 2.0 %copy-start.2 = (f32[4,8,128,256]{3,2,1,0:T(8,128)}, f32[4,8,128,256]{3,2,1,0:T(8,128)S(1)}, u32[]{:S(2)}) copy-start(f32[4,8,128,256]{3,2,1,0:T(8,128)S(1)} %get-tuple-element.20._) | copy-start | bytes 12582916
  44.4 10.3 %collective-permute-start.3 = (bf16[512,256]{1,0:T(8,128)(2,1)S(1)}, bf16[512,256]{1,0:T(8,128)(2,1)S(1)}, u32[]{:S(2)}, u32[]{:S(2)}) collective-permute-start(bf16[512,256]{1,0:T(8,128)(2,1)S(1)} %bitcast.51), channel_id=1, source_target_pairs={{0,12},{1,13},{2,14},{3,15},{16,28},{17,29},{18,30},{19,31},{32,44... | collective-permute-start | bytes 786440 | tf_op jit(solution)/shard_map/ppermute | solution.py:182
  45.7 2.2 %copy-start.3 = (f32[4,8,128,256]{3,2,1,0:T(8,128)S(1)}, f32[4,8,128,256]{3,2,1,0:T(8,128)}, u32[]{:S(2)}) copy-start(f32[4,8,128,256]{3,2,1,0:T(8,128)} %copy-done.2) | copy-start | bytes 12582916
  56.4 2.0 %copy-start.4 = (f32[4,8,128,256]{3,2,1,0:T(8,128)}, f32[4,8,128,256]{3,2,1,0:T(8,128)S(1)}, u32[]{:S(2)}) copy-start(f32[4,8,128,256]{3,2,1,0:T(8,128)S(1)} %get-tuple-element.26.acc_hbm) | copy-start | bytes 12582916
  58.4 47.0 %collective-permute-start.9 = (bf16[2,8,128,256]{3,2,1,0:T(8,128)(2,1)S(1)}, bf16[2,8,128,256]{3,2,1,0:T(8,128)(2,1)S(1)}, u32[]{:S(2)}, u32[]{:S(2)}) collective-permute-start(bf16[2,8,128,256]{3,2,1,0:T(8,128)(2,1)S(1)} %dynamic-slice_convert_fusion), channel_id=1, source_target_pairs={{0,1},{1,0},{2,3},{3,2},{4,5},{5,4},{6,7},{7,6},{8,9},{9,8},{10,11... | collective-permute-start | bytes 3145736 | tf_op jit(solution)/shard_map/ppermute | solution.py:252
  58.4 13.1 %collective-permute-start.15 = (bf16[512,256]{1,0:T(8,128)(2,1)S(1)}, bf16[512,256]{1,0:T(8,128)(2,1)S(1)}, u32[]{:S(2)}, u32[]{:S(2)}) collective-permute-start(bf16[512,256]{1,0:T(8,128)(2,1)S(1)} %get-tuple-element.33), channel_id=1, source_target_pairs={{12,0},{13,1},{14,2},{15,3},{28,16},{29,17},{30,18},{31,19},{44,32... | collective-permute-start | bytes 786440 | tf_op jit(solution)/shard_map/ppermute | solution.py:248
  59.7 13.1 %collective-permute-start.14 = (bf16[512,256]{1,0:T(8,128)(2,1)S(1)}, bf16[512,256]{1,0:T(8,128)(2,1)S(1)}, u32[]{:S(2)}, u32[]{:S(2)}) collective-permute-start(bf16[512,256]{1,0:T(8,128)(2,1)S(1)} %get-tuple-element.32), channel_id=1, source_target_pairs={{10,0},{11,1},{12,2},{13,3},{14,4},{15,5},{26,16},{27,17},{28,18},... | collective-permute-start | bytes 786440 | tf_op jit(solution)/shard_map/ppermute | solution.py:248
  61.0 13.1 %collective-permute-start.13 = (bf16[512,256]{1,0:T(8,128)(2,1)S(1)}, bf16[512,256]{1,0:T(8,128)(2,1)S(1)}, u32[]{:S(2)}, u32[]{:S(2)}) collective-permute-start(bf16[512,256]{1,0:T(8,128)(2,1)S(1)} %get-tuple-element.31), channel_id=1, source_target_pairs={{8,0},{9,1},{10,2},{11,3},{12,4},{13,5},{14,6},{15,7},{24,16},{25,... | collective-permute-start | bytes 786440 | tf_op jit(solution)/shard_map/ppermute | solution.py:248
  62.3 14.7 %collective-permute-start.12 = (bf16[512,256]{1,0:T(8,128)(2,1)S(1)}, bf16[512,256]{1,0:T(8,128)(2,1)S(1)}, u32[]{:S(2)}, u32[]{:S(2)}) collective-permute-start(bf16[512,256]{1,0:T(8,128)(2,1)S(1)} %get-tuple-element.30), channel_id=1, source_target_pairs={{6,0},{7,1},{8,2},{9,3},{10,4},{11,5},{12,6},{13,7},{14,8},{15,9},... | collective-permute-start | bytes 786440 | tf_op jit(solution)/shard_map/ppermute | solution.py:248
  71.5 11.2 %collective-permute-start.11 = (bf16[512,256]{1,0:T(8,128)(2,1)S(1)}, bf16[512,256]{1,0:T(8,128)(2,1)S(1)}, u32[]{:S(2)}, u32[]{:S(2)}) collective-permute-start(bf16[512,256]{1,0:T(8,128)(2,1)S(1)} %get-tuple-element.29), channel_id=1, source_target_pairs={{4,0},{5,1},{6,2},{7,3},{8,4},{9,5},{10,6},{11,7},{12,8},{13,9},{1... | collective-permute-start | bytes 786440 | tf_op jit(solution)/shard_map/ppermute | solution.py:248
  72.8 31.6 %collective-permute-start.10 = (bf16[512,256]{1,0:T(8,128)(2,1)S(1)}, bf16[512,256]{1,0:T(8,128)(2,1)S(1)}, u32[]{:S(2)}, u32[]{:S(2)}) collective-permute-start(bf16[512,256]{1,0:T(8,128)(2,1)S(1)} %get-tuple-element.28), channel_id=1, source_target_pairs={{2,0},{3,1},{4,2},{5,3},{6,4},{7,5},{8,6},{9,7},{10,8},{11,9},{12,... | collective-permute-start | bytes 786440 | tf_op jit(solution)/shard_map/ppermute | solution.py:248
  105.4 2.2 %copy-start.5 = (f32[4,8,128,256]{3,2,1,0:T(8,128)S(1)}, f32[4,8,128,256]{3,2,1,0:T(8,128)}, u32[]{:S(2)}) copy-start(f32[4,8,128,256]{3,2,1,0:T(8,128)} %copy-done.4) | copy-start | bytes 12582916

commit v2 on v0

v2 whole, which is shorter than its diff:
```python
import functools
import math

import jax
import jax.numpy as jnp
from jax import lax
from jax.experimental import pallas as pl
from jax.experimental.pallas import tpu as pltpu
from jax.sharding import PartitionSpec as P

F32 = jnp.float32
BF16 = jnp.bfloat16
LOG2E = math.log2(math.e)
ROWS = 256
MIB = 1 << 20
SPAN = 2048


def dot(a, b, dim_a, dim_b):
    return lax.dot_general(a, b, (((dim_a,), (dim_b,)), ((), ())), preferred_element_type=F32)


def attend(q, cot, lse, dots, lo, kpos, qpos, kv_ref, kt_ref, src_ref, dst_ref, dkv_ref):
    head_dim, keys = kt_ref.shape
    rows, width = q.shape
    scale = head_dim**-0.5
    key = kpos + lax.broadcasted_iota(jnp.int32, (keys, rows), 0)
    query = qpos + lax.broadcasted_iota(jnp.int32, (1, rows), 1)
    allowed = (key >= lo) & (key <= query)
    lse2 = lse * LOG2E
    k = kv_ref[:, :head_dim]
    v = kv_ref[:, head_dim:]
    dk = jnp.zeros((keys, head_dim), F32)
    dv = jnp.zeros((keys, head_dim), F32)
    for h in range(width // head_dim):
        cols = slice(h * head_dim, (h + 1) * head_dim)
        qh = q[:, cols]
        oh = cot[:, cols]
        scores = dot(k, qh, 1, 1)
        prob_grad = dot(v, oh, 1, 1)
        probs = jnp.where(allowed, jnp.exp2(scores * (scale * LOG2E) - lse2[h : h + 1]), 0.0)
        score_low = (probs * (prob_grad - dots[h : h + 1])).astype(BF16)
        probs_low = probs.astype(BF16)
        dv += dot(probs_low, oh, 1, 0)
        dk += dot(score_low, qh, 1, 0)
        part = dot(kt_ref[...], score_low, 1, 0)
        dst_ref[h] = part if src_ref is None else src_ref[h] + part
    dkv_ref[:, :head_dim] += dk * scale
    dkv_ref[:, head_dim:] += dv


def kernel(names, jobs, *refs):
    r = dict(zip(names, refs))
    marks, kt, dkv = r["marks"], r["kt"], r["dkv"]
    head_dim, keys = kt.shape
    per = keys // ROWS
    chip, core = marks[0], marks[1]
    chip_pos = chip * (2 * keys)
    written = set()
    for back in sorted({back for _, back in jobs}):
        kpos = (chip - back) * (2 * keys) + core * keys
        groups = [who for who, at in jobs if at == back]
        kv_ref = r[f"kv{back}"]
        counts = []
        for who in groups:
            block = core if who == "own" else 1 - core
            count = 0
            for g in range(per):
                count = count + (marks[2 + block * per + g] < kpos + keys).astype(jnp.int32)
            if back == 0:
                count = per if who == "own" else jnp.where(core == 0, count, 0)
            else:
                count = jnp.where(kpos >= 0, count, 0)
            counts.append(count)
        kt[...] = kv_ref[:, :head_dim].T
        first = back == min(at for _, at in jobs)
        dkv[...] = r["dkv_in"][...] if first and "dkv_in" in r else jnp.zeros_like(dkv)
        for who, count in zip(groups, counts):
            block = core if who == "own" else 1 - core
            dst = r[f"acc_out_{who}"]
            src = dst if who in written else r.get(f"acc_in_{who}")
            written.add(who)

            def step(g, unused, who=who, block=block, dst=dst, src=src, kpos=kpos, kv_ref=kv_ref):
                rows = pl.ds(pl.multiple_of(g * ROWS, ROWS), ROWS)
                at = block * per + g
                here = pl.ds(pl.multiple_of(at * ROWS, ROWS), ROWS)
                attend(r[f"q_{who}"].at[rows], r[f"cot_{who}"].at[rows], r[f"lse_{who}"][:, rows],
                       r[f"dots_{who}"][:, rows], r["lo"][0:1, here], kpos, chip_pos + at * ROWS,
                       kv_ref, kt, None if src is None else src.at[g], dst.at[g], dkv)
                return unused

            def skip(g, unused, dst=dst, src=src):
                if src is None:
                    dst[g] = jnp.zeros(dst.shape[1:], F32)
                else:
                    dst[g] = src[g]
                return unused

            lax.fori_loop(0, count, step, 0)
            if src is not dst:
                lax.fori_loop(count, per, skip, 0)
        out = r[f"dkv_out{back}"]
        out[...] = dkv[...].astype(out.dtype)
    if "give" in r:
        r["give"][...] = r["acc_out_other"][...].astype(BF16)
    if "sum_out" in r:
        r["sum_out"][...] = r["sum_in"][...] + r["part"][...].astype(F32)


def far_kernel(names, dists, *refs):
    r = dict(zip(names, refs))
    marks, kt, dkv, kvs = r["marks"], r["kt"], r["dkv"], r["kvs"]
    head_dim, keys = kt.shape
    per = keys // ROWS
    chip, core = marks[0], marks[1]
    chip_pos = chip * (2 * keys)
    dkv[...] = jnp.zeros_like(dkv)
    for who in ("own", "other"):
        r[f"acc_out_{who}"][...] = r[f"acc_in_{who}"][...]
    for n, d in enumerate(dists):
        @pl.when((chip >= d) & (marks[2] < (chip - d) * (2 * keys) + (core + 1) * keys))
        def _():
            kvs[n] = r[f"kv{d}"][...]

    def block_of_keys(n, unused):
        kpos = (chip - (n + dists[0])) * (2 * keys) + core * keys

        @pl.when((kpos >= 0) & (marks[2] < kpos + keys))
        def _():
            kt[...] = kvs[n, :, :head_dim].T
            for who in ("own", "other"):
                block = core if who == "own" else 1 - core
                count = 0
                for g in range(per):
                    count = count + (marks[2 + block * per + g] < kpos + keys).astype(jnp.int32)

                def step(g, unused, who=who, block=block):
                    rows = pl.ds(pl.multiple_of(g * ROWS, ROWS), ROWS)
                    at = block * per + g
                    here = pl.ds(pl.multiple_of(at * ROWS, ROWS), ROWS)
                    dst = r[f"acc_out_{who}"].at[g]
                    attend(r[f"q_{who}"].at[rows], r[f"cot_{who}"].at[rows],
                           r[f"lse_{who}"][:, rows], r[f"dots_{who}"][:, rows], r["lo"][0:1, here],
                           kpos, chip_pos + at * ROWS, kvs.at[n], kt, dst, dst, dkv.at[n])
                    return unused

                lax.fori_loop(0, count, step, 0)

        return unused

    lax.fori_loop(0, len(dists), block_of_keys, 0)
    for n, d in enumerate(dists):
        r[f"dkv_out{d}"][...] = dkv[n].astype(BF16)
    r["give"][...] = r["acc_out_other"][...].astype(BF16)


def finish_kernel(mine_ref, got_ref, out_ref):
    per, heads, head_dim = got_ref.shape[:3]
    scale = head_dim**-0.5
    for g in range(per):
        for h in range(heads):
            part = (mine_ref[g, h] + got_ref[g, h].astype(F32)) * scale
            out_ref[g * ROWS : (g + 1) * ROWS, h * head_dim : (h + 1) * head_dim] = part.T.astype(BF16)


def pack_grads(n_dev, reach, always, q, kv, cot, lse, dots, marks, lo, pack_reach):
    tok, width = q.shape
    head_dim = kv.shape[1] // 2
    heads = width // head_dim
    per = tok // ROWS
    cores = [(i, i ^ 1) for i in range(n_dev)]
    vmem = pl.BlockSpec(memory_space=pltpu.VMEM)
    smem = pl.BlockSpec(memory_space=pltpu.SMEM)
    acc32 = jax.ShapeDtypeStruct((per, heads, head_dim, ROWS), F32)
    acc16 = jax.ShapeDtypeStruct((per, heads, head_dim, ROWS), BF16)
    part32 = jax.ShapeDtypeStruct((tok, 2 * head_dim), F32)
    part16 = jax.ShapeDtypeStruct((tok, 2 * head_dim), BF16)
    tile_flops = 5 * 2 * tok * tok * width

    have = {"marks": marks, "lo": lo, "kv0": kv}
    for name, mine in (("lse", lse), ("dots", dots), ("q", q), ("cot", cot)):
        have[name + "_own"] = mine
        have[name + "_other"] = lax.ppermute(mine, "ctx", cores)
    for d in range(1, reach + 1):
        pairs = [(i, i + 2 * d) for i in range(n_dev - 2 * d)]
        have[f"kv{d}"] = lax.ppermute(kv, "ctx", pairs)

    def call(name, jobs, tiles, extra, outs):
        groups = sorted({who for who, _ in jobs})
        ins = {"marks": marks, "lo": lo}
        for who in groups:
            for part in ("lse", "dots", "q", "cot"):
                ins[f"{part}_{who}"] = have[f"{part}_{who}"]
        for back in sorted({back for _, back in jobs}):
            ins[f"kv{back}"] = have[f"kv{back}"]
        ins.update(extra)
        names = list(ins) + list(outs) + ["kt", "dkv"]
        part = (tok, 2 * head_dim)
        scratch = [pltpu.VMEM((head_dim, tok), BF16), pltpu.VMEM(part, F32)]
        body = functools.partial(kernel, names, jobs)
        if name == "far":
            dists = sorted({back for _, back in jobs})
            names += ["kvs", "acc_out_other"]
            body = functools.partial(far_kernel, names, dists)
            scratch = [scratch[0], pltpu.VMEM((len(dists),) + part, F32), pltpu.VMEM((len(dists),) + part, BF16)]
            scratch.append(pltpu.VMEM(acc32.shape, F32))
        got = pl.pallas_call(
            body,
            out_shape=tuple(outs.values()),
            in_specs=[smem] + [vmem] * (len(ins) - 1),
            out_specs=(vmem,) * len(outs),
            scratch_shapes=scratch,
            compiler_params=pltpu.CompilerParams(vmem_limit_bytes=14 * MIB),
            cost_estimate=pl.CostEstimate(
                flops=int(2 * tiles * tile_flops), bytes_accessed=4 * MIB, transcendentals=0
            ),
            name=name,
        )(*ins.values())
        return dict(zip(outs, got))

    def send(dkv, d):
        return lax.ppermute(dkv, "ctx", [(i + 2 * d, i) for i in range(n_dev - 2 * d)])

    got = call("own", [("own", 0)], 0.2, {}, {"acc_out_own": acc32, "dkv_out0": part32})
    own, total = got["acc_out_own"], got["dkv_out0"]
    got = call(
        "near", [("other", 0), ("own", 1), ("other", 1)], 0.5, {"acc_in_own": own, "dkv_in": total},
        {"acc_out_own": acc32, "acc_out_other": acc32, "dkv_out0": part32, "dkv_out1": part16},
    )
    own, other, total = got["acc_out_own"], got["acc_out_other"], got["dkv_out0"]
    parts = [send(got["dkv_out1"], 1)]

    def adding(extra, outs):
        if len(parts) > 1:
            extra.update(sum_in=total, part=parts.pop(0))
            outs["sum_out"] = part32

    for d in range(2, always + 1):
        extra = {"acc_in_own": own, "acc_in_other": other}
        outs = {"acc_out_own": acc32, "acc_out_other": acc32, f"dkv_out{d}": part16}
        adding(extra, outs)
        got = call(f"back_{d}", [("own", d), ("other", d)], 1, extra, outs)
        own, other, total = got["acc_out_own"], got["acc_out_other"], got.get("sum_out", total)
        parts.append(send(got[f"dkv_out{d}"], d))
    far = range(always + 1, reach + 1)
    extra = {"acc_in_own": own, "acc_in_other": other}
    outs = {"acc_out_own": acc32, "give": acc16}
    outs.update({f"dkv_out{d}": part16 for d in far})
    got = call("far", [(who, d) for d in far for who in ("own", "other")], 1, extra, outs)
    swapped = lax.ppermute(got["give"], "ctx", cores)

    def more(most):
        out = jnp.zeros(part32.shape, F32)
        for d in range(always + 1, most + 1):
            out = out + send(got[f"dkv_out{d}"], d).astype(F32)
        return out

    branches = [functools.partial(more, d) for d in range(always, reach + 1)]
    rest = lax.switch(jnp.clip(pack_reach - always, 0, reach - always), branches)
    grad_q = pl.pallas_call(
        finish_kernel,
        out_shape=jax.ShapeDtypeStruct((tok, width), BF16),
        in_specs=[vmem, vmem],
        out_specs=vmem,
        compiler_params=pltpu.CompilerParams(vmem_limit_bytes=16 * MIB),
        cost_estimate=pl.CostEstimate(flops=2 * MIB, bytes_accessed=4 * MIB, transcendentals=0),
        name="finish",
    )(got["acc_out_own"], swapped)
    grad_kv = total + rest
    for part in parts:
        grad_kv = grad_kv + part.astype(F32)
    return grad_q[None], grad_kv.astype(BF16)[None]


def per_device(n_dev, queries, keys_values, grad_out, log_norms, out_dots, doc_ids):
    tok = queries.shape[1]
    seq = doc_ids.shape[1]
    chip_tok = 2 * tok
    q, kv, cot, lse, dots = queries[0], keys_values[0], grad_out[0], log_norms[0], out_dots[0]
    me = lax.axis_index("ctx").astype(jnp.int32)
    chip, core = me // 2, me % 2
    lo = lax.dynamic_slice_in_dim(doc_ids, chip * chip_tok, chip_tok, 1)
    marks = jnp.concatenate([jnp.stack([chip, core]), lo[0, ::ROWS]])
    most = min(n_dev // 2 - 1, -(-(seq - SPAN - 2) // chip_tok))
    firsts = doc_ids[0, ::chip_tok] // chip_tok
    pack_reach = jnp.max(jnp.arange(n_dev // 2, dtype=jnp.int32) - firsts)
    return pack_grads(n_dev, most, min(3, most), q, kv, cot, lse, dots, marks, lo, pack_reach)


def solution(mesh):
    in_specs = (
        P("pair", "ctx", None),
        P("pair", "ctx", None),
        P("pair", "ctx", None),
        P("pair", None, "ctx"),
        P("pair", None, "ctx"),
        P("pair", None),
    )
    out_specs = (P("pair", "ctx", None), P("pair", "ctx", None))
    return jax.shard_map(
        functools.partial(per_device, mesh.shape["ctx"]),
        mesh=mesh, in_specs=in_specs, out_specs=out_specs, check_vma=False,
    )
```

time: 597 us -> 97.8 us (0.16)
  the two profiles are of different devices: /device:TPU:32 before, /device:TPU:44 now
where the time goes in v2:
time: 97.8 us; the launch traced here: 96.9 us
  Pallas kernels  33.2 us (34%)
  waiting for transfers between devices  30.8 us (31%)
  starting transfers between devices  20.6 us (21%)
  local copies, waits for them, and re-layouts  7.87 us (8%)
  other arithmetic  2.82 us (3%)
  between operations  1.57 us (2%)
    pallas_call x5, Pallas kernels, call(): pl.pallas_call(body, out_shape=tuple(outs.values()), in_specs=[smem] + [v...  31.8 us
    ppermute x3, waiting for transfers between devices, send(): lax.ppermute(dkv, 'ctx', [(i + 2 * d, i) for i in range(n_dev - 2 * d)])  30.3 us
    ppermute x6, starting transfers between devices, pack_grads(): have[f'kv{d}'] = lax.ppermute(kv, 'ctx', pairs)  15.2 us
    unnamed x24, local copies, waits for them, and re-layouts  5.38 us
    ppermute x3, starting transfers between devices, send(): lax.ppermute(dkv, 'ctx', [(i + 2 * d, i) for i in range(n_dev - 2 * d)])  4.49 us
    broadcast_in_dim x1, other arithmetic, pack_grads(): return (grad_q[None], grad_kv.astype(BF16)[None])  2.09 us
  transfers between devices with their start and end apart: 14, of which 4 were waited for; matrix products, arithmetic and copies ran while one was open for 5% of the time, Pallas kernels for 31%

profile of v2, /device:TPU:44, one launch (start us, length us, event | category | flops | bytes accessed | tf_op | source)
XLA Modules:
  0.0 96.9 jit_solution(11265422871167624179)
XLA Ops:
  0.6 0.0 copy-start.9
  0.6 0.1 collective-permute-start.8
  0.7 0.5 collective-permute-start.9
  1.2 3.5 %collective-permute-start.15 = (bf16[512,256]{1,0:T(8,128)(2,1)}, bf16[512,256]{1,0:T(8,128)(2,1)S(1)}, u32[]{:S(2)}, u32[]{:S(2)}) collective-permute-start(bf16[512,256]{1,0:T(8,128)(2,1)} %bitcast.7.refs_6_.refs_10_), channel_id=1, source_target_pairs={{0,2},{1,3},{2,4},{3,5},{4,6},{5,7},{6,8},{7,9},{8,10},{9,11},{10,... | collective-permute-start | bytes 786440 | tf_op jit(solution)/shard_map/ppermute | solution.py:187
  4.7 3.5 %collective-permute-start.14 = (bf16[512,256]{1,0:T(8,128)(2,1)}, bf16[512,256]{1,0:T(8,128)(2,1)S(1)}, u32[]{:S(2)}, u32[]{:S(2)}) collective-permute-start(bf16[512,256]{1,0:T(8,128)(2,1)} %bitcast.7.refs_6_.refs_10_), channel_id=1, source_target_pairs={{0,4},{1,5},{2,6},{3,7},{4,8},{5,9},{6,10},{7,11},{8,12},{9,13},{1... | collective-permute-start | bytes 786440 | tf_op jit(solution)/shard_map/ppermute | solution.py:187
  8.2 0.1 collective-permute-start.6
  8.3 0.7 constant_dynamic-slice_fusion.refs_1_
  9.0 0.1 slice.6
  9.1 0.1 pad_add_fusion.refs_0_
  9.2 0.5 collective-permute-done.6.refs_2_
  9.7 0.2 collective-permute-start.7
  9.9 1.2 %copy-done.1 = bf16[1,512,1024]{2,1,0:T(8,128)(2,1)S(1)} copy-done((bf16[1,512,1024]{2,1,0:T(8,128)(2,1)S(1)}, bf16[1,512,1024]{2,1,0:T(8,128)(2,1)}, u32[]{:S(2)}) %copy-start.1) | copy-done | bytes 1048600
  11.1 1.2 %copy-done.3 = bf16[1,512,1024]{2,1,0:T(8,128)(2,1)S(1)} copy-done((bf16[1,512,1024]{2,1,0:T(8,128)(2,1)S(1)}, bf16[1,512,1024]{2,1,0:T(8,128)(2,1)}, u32[]{:S(2)}) %copy-start.3) | copy-done | bytes 1048600
  12.3 0.7 copy-done.8
  13.0 0.7 copy-done.10
  13.8 7.4 %own.1 = (f32[2,8,128,256]{3,2,1,0:T(8,128)S(1)}, f32[512,256]{1,0:T(8,128)S(1)}) custom-call(s32[6]{0:T(128)S(1)} %pad_add_fusion.refs_0_, s32[1,1024]{1,0:T(1,128)S(1)} %constant_dynamic-slice_fusion.refs_1_, f32[8,512]{1,0:T(8,128)S(1)} %bitcast.34, f32[8,512]{1,0:T(8,128)S(1)} %bitcast.40, bf16[512,1024]{1,0:T(8,128)(2,1)S(1)} %bitcast.22, ...), custom_call_target="tpu_custom_call" | custom-call | flops 1073741824 | bytes 4194304 | tf_op jit(solution)/shard_map/own/pallas_call | solution.py:208
  21.2 0.0 collective-permute-done.7.refs_3_
  21.2 4.3 %collective-permute-start.13 = (bf16[512,256]{1,0:T(8,128)(2,1)}, bf16[512,256]{1,0:T(8,128)(2,1)S(1)}, u32[]{:S(2)}, u32[]{:S(2)}) collective-permute-start(bf16[512,256]{1,0:T(8,128)(2,1)} %bitcast.7.refs_6_.refs_10_), channel_id=1, source_target_pairs={{0,6},{1,7},{2,8},{3,9},{4,10},{5,11},{6,12},{7,13},{8,14},{9,15},... | collective-permute-start | bytes 786440 | tf_op jit(solution)/shard_map/ppermute | solution.py:187
  25.5 0.0 collective-permute-done.15.refs_11_
  25.5 1.3 %collective-permute-start.10 = (bf16[512,256]{1,0:T(8,128)(2,1)}, bf16[512,256]{1,0:T(8,128)(2,1)S(1)}, u32[]{:S(2)}, u32[]{:S(2)}) collective-permute-start(bf16[512,256]{1,0:T(8,128)(2,1)} %bitcast.7.refs_6_.refs_10_), channel_id=1, source_target_pairs={{0,8},{1,9},{2,10},{3,11},{4,12},{5,13},{6,14},{7,15},{16,24},{17,... | collective-permute-start | bytes 786440 | tf_op jit(solution)/shard_map/ppermute | solution.py:187
  26.8 0.0 collective-permute-done.8.refs_4_
  26.9 1.3 %collective-permute-start.11 = (bf16[512,256]{1,0:T(8,128)(2,1)}, bf16[512,256]{1,0:T(8,128)(2,1)S(1)}, u32[]{:S(2)}, u32[]{:S(2)}) collective-permute-start(bf16[512,256]{1,0:T(8,128)(2,1)} %bitcast.7.refs_6_.refs_10_), channel_id=1, source_target_pairs={{0,10},{1,11},{2,12},{3,13},{4,14},{5,15},{16,26},{17,27},{18,28},... | collective-permute-start | bytes 786440 | tf_op jit(solution)/shard_map/ppermute | solution.py:187
  28.2 0.0 collective-permute-done.9.refs_5_
  28.2 0.0 copy-start.5
  28.2 1.3 %collective-permute-start.12 = (bf16[512,256]{1,0:T(8,128)(2,1)}, bf16[512,256]{1,0:T(8,128)(2,1)S(1)}, u32[]{:S(2)}, u32[]{:S(2)}) collective-permute-start(bf16[512,256]{1,0:T(8,128)(2,1)} %bitcast.7.refs_6_.refs_10_), channel_id=1, source_target_pairs={{0,12},{1,13},{2,14},{3,15},{16,28},{17,29},{18,30},{19,31},{32,44... | collective-permute-start | bytes 786440 | tf_op jit(solution)/shard_map/ppermute | solution.py:187
  29.5 0.0 copy-start.11
  29.5 20.0 %near.1 = (f32[2,8,128,256]{3,2,1,0:T(8,128)S(1)}, f32[2,8,128,256]{3,2,1,0:T(8,128)S(1)}, f32[512,256]{1,0:T(8,128)S(1)}, bf16[512,256]{1,0:T(8,128)(2,1)S(1)}) custom-call(s32[6]{0:T(128)S(1)} %pad_add_fusion.refs_0_, s32[1,1024]{1,0:T(1,128)S(1)} %constant_dynamic-slice_fusion.refs_1_, f32[8,512]{1,0:T(8,128)S(1)} %collective-permute-done.6.refs_2_, ...), custom_call_target="tpu_custom_call" | custom-call | flops 2684354560 | bytes 4194304 | tf_op jit(solution)/shard_map/near/pallas_call | solution.py:208
  49.6 1.9 %collective-permute-start.16 = (bf16[512,256]{1,0:T(8,128)(2,1)S(1)}, bf16[512,256]{1,0:T(8,128)(2,1)S(1)}, u32[]{:S(2)}, u32[]{:S(2)}) collective-permute-start(bf16[512,256]{1,0:T(8,128)(2,1)S(1)} %get-tuple-element.48), channel_id=1, source_target_pairs={{2,0},{3,1},{4,2},{5,3},{6,4},{7,5},{8,6},{9,7},{10,8},{11,9},{12,... | collective-permute-start | bytes 786440 | tf_op jit(solution)/shard_map/ppermute | solution.py:223
  51.6 0.9 back_2.1
  52.5 0.0 collective-permute-done.13.refs_10_
  52.5 5.4 %collective-permute-done.16.refs_14_ = bf16[512,256]{1,0:T(8,128)(2,1)S(1)} collective-permute-done((bf16[512,256]{1,0:T(8,128)(2,1)S(1)}, bf16[512,256]{1,0:T(8,128)(2,1)S(1)}, u32[]{:S(2)}, u32[]{:S(2)}) %collective-permute-start.16) | collective-permute-done | bytes 262176 | tf_op jit(solution)/shard_map/ppermute | solution.py:223
  57.9 1.2 %back_3.1 = (f32[2,8,128,256]{3,2,1,0:T(8,128)S(1)}, f32[2,8,128,256]{3,2,1,0:T(8,128)S(1)}, bf16[512,256]{1,0:T(8,128)(2,1)S(1)}, f32[512,256]{1,0:T(8,128)S(1)}) custom-call(s32[6]{0:T(128)S(1)} %pad_add_fusion.refs_0_, s32[1,1024]{1,0:T(1,128)S(1)} %constant_dynamic-slice_fusion.refs_1_, f32[8,512]{1,0:T(8,128)S(1)} %collective-permute-done.6.refs_2_, ...), custom_call_target="tpu_custom_call" | custom-call | flops 5368709120 | bytes 4194304 | tf_op jit(solution)/shard_map/back_3/pallas_call | solution.py:208
  59.1 0.0 collective-permute-done.10.refs_10_
  59.1 0.0 collective-permute-done.12.refs_12_
  59.1 0.0 copy-start.6
  59.2 1.5 %copy-done.6 = bf16[512,1024]{1,0:T(8,128)(2,1)S(1)} copy-done((bf16[512,1024]{1,0:T(8,128)(2,1)S(1)}, bf16[512,1024]{1,0:T(8,128)(2,1)}, u32[]{:S(2)}) %copy-start.6) | copy-done | bytes 1048600
  60.6 2.2 %far.1 = (f32[2,8,128,256]{3,2,1,0:T(8,128)S(1)}, bf16[2,8,128,256]{3,2,1,0:T(8,128)(2,1)}, bf16[512,256]{1,0:T(8,128)(2,1)}, bf16[512,256]{1,0:T(8,128)(2,1)}, bf16[512,256]{1,0:T(8,128)(2,1)}) custom-call(s32[6]{0:T(128)S(1)} %pad_add_fusion.refs_0_, s32[1,1024]{1,0:T(1,128)S(1)} %constant_dynamic-slice_fusion.refs_1_, ...), custom_call_target="tpu_custom_call" | custom-call | flops 5368709120 | bytes 4194304 | tf_op jit(solution)/shard_map/far/pallas_call | solution.py:208
  62.9 0.1 collective-permute-start.17
  63.0 0.9 slice.7
  63.8 0.7 subtract_reduce_fusion
  65.1 1.3 %collective-permute-start.18 = (bf16[512,256]{1,0:T(8,128)(2,1)S(1)}, bf16[512,256]{1,0:T(8,128)(2,1)}, u32[]{:S(2)}, u32[]{:S(2)}) collective-permute-start(bf16[512,256]{1,0:T(8,128)(2,1)S(1)} %get-tuple-element.57), channel_id=1, source_target_pairs={{4,0},{5,1},{6,2},{7,3},{8,4},{9,5},{10,6},{11,7},{12,8},{13,9},{1... | collective-permute-start | bytes 786440 | tf_op jit(solution)/shard_map/ppermute | solution.py:223
  66.4 0.9 conditional.1
  66.4 0.8 broadcast.14
  67.2 1.3 %collective-permute-start.19 = (bf16[512,256]{1,0:T(8,128)(2,1)}, bf16[512,256]{1,0:T(8,128)(2,1)S(1)}, u32[]{:S(2)}, u32[]{:S(2)}) collective-permute-start(bf16[512,256]{1,0:T(8,128)(2,1)} %copy-done.7), channel_id=1, source_target_pairs={{6,0},{7,1},{8,2},{9,3},{10,4},{11,5},{12,6},{13,7},{14,8},{15,9},... | collective-permute-start | bytes 786440 | tf_op jit(solution)/shard_map/ppermute | solution.py:223
  68.5 8.8 %collective-permute-done.18 = bf16[512,256]{1,0:T(8,128)(2,1)} collective-permute-done((bf16[512,256]{1,0:T(8,128)(2,1)S(1)}, bf16[512,256]{1,0:T(8,128)(2,1)}, u32[]{:S(2)}, u32[]{:S(2)}) %collective-permute-start.18) | collective-permute-done | bytes 262176 | tf_op jit(solution)/shard_map/ppermute | solution.py:223
  77.3 16.2 %collective-permute-done.19 = bf16[512,256]{1,0:T(8,128)(2,1)S(1)} collective-permute-done((bf16[512,256]{1,0:T(8,128)(2,1)}, bf16[512,256]{1,0:T(8,128)(2,1)S(1)}, u32[]{:S(2)}, u32[]{:S(2)}) %collective-permute-start.19) | collective-permute-done | bytes 262176 | tf_op jit(solution)/shard_map/ppermute | solution.py:223
  93.5 2.1 %fusion = bf16[1,512,256]{2,1,0:T(8,128)(2,1)} fusion(bf16[512,256]{1,0:T(8,128)(2,1)S(1)} %collective-permute-done.19, bf16[512,256]{1,0:T(8,128)(2,1)} %collective-permute-done.18, f32[512,256]{1,0:T(8,128)} %copy-done, f32[512,256]{1,0:T(8,128)} %get-tuple-element.59), kind=kLoop, calls=%fused_computation.3 | loop fusion | flops 786432 | bytes 1835008 | tf_op jit(solution)/shard_map/broadcast_in_dim | solution.py:273
  95.6 1.4 %finish.1 = bf16[512,1024]{1,0:T(8,128)(2,1)} custom-call(f32[2,8,128,256]{3,2,1,0:T(8,128)S(1)} %get-tuple-element.51.mine_ref, bf16[2,8,128,256]{3,2,1,0:T(8,128)(2,1)S(1)} %collective-permute-done.17.got_ref), custom_call_target="tpu_custom_call" | custom-call | flops 2097152 | bytes 4194304 | tf_op jit(solution)/shard_map/finish/pallas_call | solution.py:261
  (18 shorter events, 0.0 us)
Async XLA Ops:
  0.6 28.9 %copy-start.9 = (f32[1,8,512]{2,1,0:T(8,128)S(1)}, f32[1,8,512]{2,1,0:T(8,128)}, u32[]{:S(2)}) copy-start(f32[1,8,512]{2,1,0:T(8,128)} %param.13) | copy-start | bytes 49156
  0.6 26.2 %collective-permute-start.8 = (bf16[512,1024]{1,0:T(8,128)(2,1)}, bf16[512,1024]{1,0:T(8,128)(2,1)S(1)}, u32[]{:S(2)}, u32[]{:S(2)}) collective-permute-start(bf16[512,1024]{1,0:T(8,128)(2,1)} %bitcast.21), channel_id=1, source_target_pairs={{0,1},{1,0},{2,3},{3,2},{4,5},{5,4},{6,7},{7,6},{8,9},{9,8},{10,11... | collective-permute-start | bytes 3145736 | tf_op jit(solution)/shard_map/ppermute | solution.py:184
  0.7 27.4 %collective-permute-start.9 = (bf16[512,1024]{1,0:T(8,128)(2,1)}, bf16[512,1024]{1,0:T(8,128)(2,1)S(1)}, u32[]{:S(2)}, u32[]{:S(2)}) collective-permute-start(bf16[512,1024]{1,0:T(8,128)(2,1)} %bitcast.27), channel_id=1, source_target_pairs={{0,1},{1,0},{2,3},{3,2},{4,5},{5,4},{6,7},{7,6},{8,9},{9,8},{10,11... | collective-permute-start | bytes 3145736 | tf_op jit(solution)/shard_map/ppermute | solution.py:184
  1.2 24.3 %collective-permute-start.15 = (bf16[512,256]{1,0:T(8,128)(2,1)}, bf16[512,256]{1,0:T(8,128)(2,1)S(1)}, u32[]{:S(2)}, u32[]{:S(2)}) collective-permute-start(bf16[512,256]{1,0:T(8,128)(2,1)} %bitcast.7.refs_6_.refs_10_), channel_id=1, source_target_pairs={{0,2},{1,3},{2,4},{3,5},{4,6},{5,7},{6,8},{7,9},{8,10},{9,11},{10,... | collective-permute-start | bytes 786440 | tf_op jit(solution)/shard_map/ppermute | solution.py:187
  4.7 44.9 %collective-permute-start.14 = (bf16[512,256]{1,0:T(8,128)(2,1)}, bf16[512,256]{1,0:T(8,128)(2,1)S(1)}, u32[]{:S(2)}, u32[]{:S(2)}) collective-permute-start(bf16[512,256]{1,0:T(8,128)(2,1)} %bitcast.7.refs_6_.refs_10_), channel_id=1, source_target_pairs={{0,4},{1,5},{2,6},{3,7},{4,8},{5,9},{6,10},{7,11},{8,12},{9,13},{1... | collective-permute-start | bytes 786440 | tf_op jit(solution)/shard_map/ppermute | solution.py:187
  8.2 1.5 %collective-permute-start.6 = (f32[8,512]{1,0:T(8,128)}, f32[8,512]{1,0:T(8,128)S(1)}, u32[]{:S(2)}, u32[]{:S(2)}) collective-permute-start(f32[8,512]{1,0:T(8,128)} %bitcast.33), channel_id=1, source_target_pairs={{0,1},{1,0},{2,3},{3,2},{4,5},{5,4},{6,7},{7,6},{8,9},{9,8},{10,11... | collective-permute-start | bytes 49160 | tf_op jit(solution)/shard_map/ppermute | solution.py:184
  9.7 11.5 %collective-permute-start.7 = (f32[8,512]{1,0:T(8,128)}, f32[8,512]{1,0:T(8,128)S(1)}, u32[]{:S(2)}, u32[]{:S(2)}) collective-permute-start(f32[8,512]{1,0:T(8,128)} %bitcast.39), channel_id=1, source_target_pairs={{0,1},{1,0},{2,3},{3,2},{4,5},{5,4},{6,7},{7,6},{8,9},{9,8},{10,11... | collective-permute-start | bytes 49160 | tf_op jit(solution)/shard_map/ppermute | solution.py:184
  9.9 1.2 %copy-start.1 = (bf16[1,512,1024]{2,1,0:T(8,128)(2,1)S(1)}, bf16[1,512,1024]{2,1,0:T(8,128)(2,1)}, u32[]{:S(2)}) copy-start(bf16[1,512,1024]{2,1,0:T(8,128)(2,1)} %param.10) | copy-start | bytes 3145732
  11.1 1.2 %copy-start.3 = (bf16[1,512,1024]{2,1,0:T(8,128)(2,1)S(1)}, bf16[1,512,1024]{2,1,0:T(8,128)(2,1)}, u32[]{:S(2)}) copy-start(bf16[1,512,1024]{2,1,0:T(8,128)(2,1)} %param.12) | copy-start | bytes 3145732
  12.3 0.7 copy-start.8
  13.0 0.7 copy-start.10
  13.8 15.8 %copy-start.2 = (bf16[1,512,1024]{2,1,0:T(8,128)(2,1)S(1)}, bf16[1,512,1024]{2,1,0:T(8,128)(2,1)}, u32[]{:S(2)}) copy-start(bf16[1,512,1024]{2,1,0:T(8,128)(2,1)} %param.10) | copy-start | bytes 3145732
  13.8 15.8 %copy-start.4 = (bf16[1,512,1024]{2,1,0:T(8,128)(2,1)S(1)}, bf16[1,512,1024]{2,1,0:T(8,128)(2,1)}, u32[]{:S(2)}) copy-start(bf16[1,512,1024]{2,1,0:T(8,128)(2,1)} %param.12) | copy-start | bytes 3145732
  21.2 31.3 %collective-permute-start.13 = (bf16[512,256]{1,0:T(8,128)(2,1)}, bf16[512,256]{1,0:T(8,128)(2,1)S(1)}, u32[]{:S(2)}, u32[]{:S(2)}) collective-permute-start(bf16[512,256]{1,0:T(8,128)(2,1)} %bitcast.7.refs_6_.refs_10_), channel_id=1, source_target_pairs={{0,6},{1,7},{2,8},{3,9},{4,10},{5,11},{6,12},{7,13},{8,14},{9,15},... | collective-permute-start | bytes 786440 | tf_op jit(solution)/shard_map/ppermute | solution.py:187
  25.5 33.6 %collective-permute-start.10 = (bf16[512,256]{1,0:T(8,128)(2,1)}, bf16[512,256]{1,0:T(8,128)(2,1)S(1)}, u32[]{:S(2)}, u32[]{:S(2)}) collective-permute-start(bf16[512,256]{1,0:T(8,128)(2,1)} %bitcast.7.refs_6_.refs_10_), channel_id=1, source_target_pairs={{0,8},{1,9},{2,10},{3,11},{4,12},{5,13},{6,14},{7,15},{16,24},{17,... | collective-permute-start | bytes 786440 | tf_op jit(solution)/shard_map/ppermute | solution.py:187
  26.9 32.3 %collective-permute-start.11 = (bf16[512,256]{1,0:T(8,128)(2,1)}, bf16[512,256]{1,0:T(8,128)(2,1)S(1)}, u32[]{:S(2)}, u32[]{:S(2)}) collective-permute-start(bf16[512,256]{1,0:T(8,128)(2,1)} %bitcast.7.refs_6_.refs_10_), channel_id=1, source_target_pairs={{0,10},{1,11},{2,12},{3,13},{4,14},{5,15},{16,26},{17,27},{18,28},... | collective-permute-start | bytes 786440 | tf_op jit(solution)/shard_map/ppermute | solution.py:187
  28.2 29.7 %copy-start.5 = (bf16[512,1024]{1,0:T(8,128)(2,1)}, bf16[512,1024]{1,0:T(8,128)(2,1)S(1)}, u32[]{:S(2)}) copy-start(bf16[512,1024]{1,0:T(8,128)(2,1)S(1)} %collective-permute-done.9.refs_5_) | copy-start | bytes 3145732
  28.2 30.9 %collective-permute-start.12 = (bf16[512,256]{1,0:T(8,128)(2,1)}, bf16[512,256]{1,0:T(8,128)(2,1)S(1)}, u32[]{:S(2)}, u32[]{:S(2)}) collective-permute-start(bf16[512,256]{1,0:T(8,128)(2,1)} %bitcast.7.refs_6_.refs_10_), channel_id=1, source_target_pairs={{0,12},{1,13},{2,14},{3,15},{16,28},{17,29},{18,30},{19,31},{32,44... | collective-permute-start | bytes 786440 | tf_op jit(solution)/shard_map/ppermute | solution.py:187
  29.5 22.0 %copy-start.11 = (f32[1,8,512]{2,1,0:T(8,128)S(1)}, f32[1,8,512]{2,1,0:T(8,128)}, u32[]{:S(2)}) copy-start(f32[1,8,512]{2,1,0:T(8,128)} %param.14) | copy-start | bytes 49156
  49.6 8.3 %collective-permute-start.16 = (bf16[512,256]{1,0:T(8,128)(2,1)S(1)}, bf16[512,256]{1,0:T(8,128)(2,1)S(1)}, u32[]{:S(2)}, u32[]{:S(2)}) collective-permute-start(bf16[512,256]{1,0:T(8,128)(2,1)S(1)} %get-tuple-element.48), channel_id=1, source_target_pairs={{2,0},{3,1},{4,2},{5,3},{6,4},{7,5},{8,6},{9,7},{10,8},{11,9},{12,... | collective-permute-start | bytes 786440 | tf_op jit(solution)/shard_map/ppermute | solution.py:223
  59.1 3.8 %copy-start = (f32[512,256]{1,0:T(8,128)}, f32[512,256]{1,0:T(8,128)S(1)}, u32[]{:S(2)}) copy-start(f32[512,256]{1,0:T(8,128)S(1)} %get-tuple-element.53) | copy-start | bytes 1572868
  59.1 3.7 %copy-start.7 = (bf16[512,256]{1,0:T(8,128)(2,1)}, bf16[512,256]{1,0:T(8,128)(2,1)S(1)}, u32[]{:S(2)}) copy-start(bf16[512,256]{1,0:T(8,128)(2,1)S(1)} %get-tuple-element.58) | copy-start | bytes 786436
  59.1 1.5 %copy-start.6 = (bf16[512,1024]{1,0:T(8,128)(2,1)S(1)}, bf16[512,1024]{1,0:T(8,128)(2,1)}, u32[]{:S(2)}) copy-start(bf16[512,1024]{1,0:T(8,128)(2,1)} %copy-done.5) | copy-start | bytes 3145732
  62.9 32.7 %collective-permute-start.17 = (bf16[2,8,128,256]{3,2,1,0:T(8,128)(2,1)}, bf16[2,8,128,256]{3,2,1,0:T(8,128)(2,1)S(1)}, u32[]{:S(2)}, u32[]{:S(2)}) collective-permute-start(bf16[2,8,128,256]{3,2,1,0:T(8,128)(2,1)} %get-tuple-element.52), channel_id=1, source_target_pairs={{0,1},{1,0},{2,3},{3,2},{4,5},{5,4},{6,7},{7,6},{8,9},{9,8},{10,11... | collective-permute-start | bytes 3145736 | tf_op jit(solution)/shard_map/ppermute | solution.py:251
  65.1 12.2 %collective-permute-start.18 = (bf16[512,256]{1,0:T(8,128)(2,1)S(1)}, bf16[512,256]{1,0:T(8,128)(2,1)}, u32[]{:S(2)}, u32[]{:S(2)}) collective-permute-start(bf16[512,256]{1,0:T(8,128)(2,1)S(1)} %get-tuple-element.57), channel_id=1, source_target_pairs={{4,0},{5,1},{6,2},{7,3},{8,4},{9,5},{10,6},{11,7},{12,8},{13,9},{1... | collective-permute-start | bytes 786440 | tf_op jit(solution)/shard_map/ppermute | solution.py:223
  67.2 26.2 %collective-permute-start.19 = (bf16[512,256]{1,0:T(8,128)(2,1)}, bf16[512,256]{1,0:T(8,128)(2,1)S(1)}, u32[]{:S(2)}, u32[]{:S(2)}) collective-permute-start(bf16[512,256]{1,0:T(8,128)(2,1)} %copy-done.7), channel_id=1, source_target_pairs={{6,0},{7,1},{8,2},{9,3},{10,4},{11,5},{12,6},{13,7},{14,8},{15,9},... | collective-permute-start | bytes 786440 | tf_op jit(solution)/shard_map/ppermute | solution.py:223
